TPU v7x, 32 devices: a whole 2x2x4 slice. The times are simulated.
32 devices in a mesh: fsdp: 8 (over y, x, core), tp: 4 (over z).
Axes of the slice: x: 2, y: 2, z: 4, core: 2. Of those that a mesh axis runs over, the one named last changes fastest.
Arguments:
- roll_rows: bfloat16 [256, 72, 3584], P('fsdp', None, 'tp'), may hold values from -60 to 60
- dest: int32 [256], P('fsdp'), may hold values from 0 to 255, as said below
- lengths: int32 [8, 32], P('fsdp'), may hold values from 1 to 72, 768 in all within a row
- clusters: int32 [256], P('fsdp'), may hold values from 0 to 3
- log_prob_grad: bfloat16 [6144, 3584], P('fsdp', 'tp'), may hold values from -6 to 6
- gain: bfloat16 [3584], replicated, may hold values from 0.5 to 1.5
- w_q: bfloat16 [3584, 2048], P('fsdp', 'tp'), may hold values from -1 to 1
- w_k: bfloat16 [3584, 512], P('fsdp', 'tp'), may hold values from -1 to 1
- w_v: bfloat16 [3584, 512], P('fsdp', 'tp'), may hold values from -0.09375 to 0.09375
- w_o_t: bfloat16 [3584, 2048], P('fsdp', 'tp'), may hold values from -0.125 to 0.125
Outputs:
- input_grad: bfloat16 [6144, 3584], P('fsdp', 'tp')
- grad_q: bfloat16 [3584, 2048], P('fsdp', 'tp')
- grad_k: bfloat16 [3584, 512], P('fsdp', 'tp')
- grad_v: bfloat16 [3584, 512], P('fsdp', 'tp')
- grad_o_t: bfloat16 [3584, 2048], P('fsdp', 'tp')
Inputs may be any that keep to these rules, and one draw needn't show every extreme that they name: dest is a permutation; every rollout replica hands exactly 4 completions to every learner, and every learner trains 32 completions. Each learner's 32 lengths sum to 768.
All inputs are finite; a program needn't handle non-finite values.
Results may differ from a plain program's by a relative error of at most 0.03.
Values may be sent and summed in bfloat16 or wider, within the bound.
No kernel may reach another device: no remote copies, remote signals or barrier semaphores. Data moves between devices by JAX's collectives and lax.ppermute only.
A program may use at most 128 MiB of HBM per device.

v0:
```python
import functools

import jax
import jax.numpy as jnp
from jax import lax
from jax.experimental import pallas as pl
from jax.experimental.pallas import tpu as pltpu
from jax.sharding import PartitionSpec as P

KEY_VALUE_HEADS = 4
HD = 128
QUERY_HEADS = 16
GSIZE = 16
ROPE_BASE = 1000000.0
NORM_EPSILON = 1e-06
BLOCK = 128

UP = [(0, 1), (1, 2), (2, 3)]
DOWN = [(1, 0), (2, 1), (3, 2)]
UP_MID = [(1, 2), (2, 3)]
DOWN_MID = [(1, 0), (2, 1)]
TO_ENDS = [(2, 3), (1, 0)]
FROM_ENDS = [(3, 2), (0, 1)]
UP_IN = [(0, 1), (1, 2)]
DOWN_IN = [(3, 2), (2, 1)]


def contract_rows(left, right):
    return lax.dot_general(
        left, right, (((0,), (0,)), ((), ())), preferred_element_type=jnp.float32
    )


def times_trans(left, right):
    return lax.dot_general(
        left, right, (((1,), (1,)), ((), ())), preferred_element_type=jnp.float32
    )


def matmul(left, right):
    return jnp.dot(left, right, preferred_element_type=jnp.float32)


def gather_near(own):
    return lax.ppermute(own, "tp", UP), lax.ppermute(own, "tp", DOWN)


def gather_far(step1, z):
    up2 = lax.ppermute(step1[0], "tp", UP_MID)
    down2 = lax.ppermute(step1[1], "tp", DOWN_MID)
    return jnp.where(z >= 2, up2, down2)


def gather_end(far2):
    return lax.ppermute(far2, "tp", TO_ENDS)


def shards(own, step1, far2, far3, z):
    up1, down1 = step1
    near = jnp.where(z % 2 == 1, up1, down1)
    other = jnp.where(z == 1, down1, jnp.where(z == 2, up1, far3))
    return [own, near, far2, other]


def after(value, *earlier):
    return lax.optimization_barrier((value, *earlier))[0]


def scatter_end(parts):
    return lax.ppermute(parts[3], "tp", FROM_ENDS)


def far_total(parts, from_end):
    return (parts[2].astype(jnp.float32) + from_end.astype(jnp.float32)).astype(jnp.bfloat16)


def scatter_far(total2):
    return lax.ppermute(total2, "tp", UP_IN), lax.ppermute(total2, "tp", DOWN_IN)


def scatter_near(parts, step2, z):
    own, near, _, other = parts
    f32 = jnp.float32
    up2, down2 = step2
    go_up = jnp.where(z == 1, other, near).astype(f32) + up2.astype(f32)
    go_down = jnp.where(z == 2, other, near).astype(f32) + down2.astype(f32)
    up3 = lax.ppermute(go_up.astype(jnp.bfloat16), "tp", UP)
    down3 = lax.ppermute(go_down.astype(jnp.bfloat16), "tp", DOWN)
    return own.astype(f32) + up3.astype(f32) + down3.astype(f32)


def attention_kernel(*refs):
    raw_refs, inv_refs, ga_refs = refs[:2], refs[2:4], refs[4:6]
    adv_ref, cos_ref, sin_ref, start_ref = refs[6:10]
    dqkv_refs, scale_refs = refs[10:12], refs[12:14]
    dscaled_ref, out_ref, qkv_b, dq_b, dk_acc, dv_acc = refs[14:]
    heads = ga_refs[0].shape[1] // HD
    qw = heads * HD
    scale = HD ** (-0.5)
    f32, bf16 = jnp.float32, jnp.bfloat16
    blocks = adv_ref.shape[0] // BLOCK

    def span(block):
        return slice(block * BLOCK, (block + 1) * BLOCK)

    def piece(pair, block):
        first = pair[0].shape[0] // BLOCK
        return (pair[0], span(block)) if block < first else (pair[1], span(block - first))

    def read(pair, block, cols):
        ref, rows = piece(pair, block)
        return ref[rows, cols]

    def turn(value, cos, sin):
        return value * cos + pltpu.roll(value, HD // 2, 1) * sin

    def inverse(block):
        return read(inv_refs, block, slice(0, 1))

    qkv_b[span(0), :] = jnp.zeros((BLOCK, qkv_b.shape[1]), bf16)
    dk_acc[span(0), :] = jnp.zeros((BLOCK, HD), f32)
    dv_acc[span(0), :] = jnp.zeros((BLOCK, HD), f32)

    for block in range(blocks):
        here, after = span(block), span(block + 1)
        both = slice(block * BLOCK, (block + 2) * BLOCK)
        cos, sin = cos_ref[here, :], sin_ref[here, :]
        inv = inverse(block)
        for h in range(heads + 2):
            cols = slice(h * HD, (h + 1) * HD)
            linear = read(raw_refs, block, cols) * inv
            qkv_b[after, cols] = (turn(linear, cos, sin) if h <= heads else linear).astype(bf16)
        adv = adv_ref[here, :]
        qs = jnp.concatenate(
            [qkv_b[after, h * HD : (h + 1) * HD] for h in range(heads)], axis=0
        )
        gs = jnp.concatenate(
            [
                (read(ga_refs, block, slice(h * HD, (h + 1) * HD)) * adv).astype(bf16)
                for h in range(heads)
            ],
            axis=0,
        )
        ks = qkv_b[both, qw : qw + HD]
        vs = qkv_b[both, qw + HD : qw + 2 * HD]
        start = start_ref[here, :] - (block - 1) * BLOCK
        col = lax.broadcasted_iota(jnp.int32, (BLOCK, 2 * BLOCK), 1)
        row = lax.broadcasted_iota(jnp.int32, (BLOCK, 2 * BLOCK), 0) + BLOCK
        bias = jnp.where((col >= start) & (col <= row), 0.0, -1e30)
        bias = jnp.concatenate([bias] * heads, axis=0)
        scores = times_trans(qs, ks) * scale + bias
        top = jnp.max(scores, axis=-1, keepdims=True)
        weight = jnp.exp(scores - top)
        prob = weight / jnp.sum(weight, axis=-1, keepdims=True)
        prob_b = prob.astype(bf16)
        out = matmul(prob_b, vs)
        grad_prob = times_trans(gs, vs)
        delta = jnp.sum(prob * grad_prob, axis=-1, keepdims=True)
        ds = (prob * (grad_prob - delta) * scale).astype(bf16)
        dq = matmul(ds, ks)
        dk_acc[here, :] += contract_rows(ds[:, :BLOCK], qs)
        dk_acc[after, :] = contract_rows(ds[:, BLOCK:], qs)
        dv_acc[here, :] += contract_rows(prob_b[:, :BLOCK], gs)
        dv_acc[after, :] = contract_rows(prob_b[:, BLOCK:], gs)
        for h in range(heads):
            cols = slice(h * HD, (h + 1) * HD)
            out_ref[here, cols] = (out[span(h), :].astype(bf16).astype(f32) * adv).astype(bf16)
            dq_b[here, cols] = turn(dq[span(h), :], cos, -sin).astype(bf16)

    for block in range(blocks):
        here, after = span(block), span(block + 1)
        cos, sin = cos_ref[here, :], sin_ref[here, :]
        inv = inverse(block)
        dqkv_ref, to = piece(dqkv_refs, block)
        total = jnp.zeros((BLOCK, 1), f32)
        for h in range(heads + 2):
            cols = slice(h * HD, (h + 1) * HD)
            if h < heads:
                grad = dq_b[here, cols]
            elif h == heads:
                grad = turn(dk_acc[after, :], cos, -sin).astype(bf16)
            else:
                grad = dv_acc[after, :].astype(bf16)
            dqkv_ref[to, cols] = grad
            grad = grad.astype(f32) * inv
            dscaled_ref[here, cols] = grad.astype(bf16)
            total += jnp.sum(grad * read(raw_refs, block, cols), axis=-1, keepdims=True)
        scale_ref, to = piece(scale_refs, block)
        scale_ref[to, 0:1] = inv
        scale_ref[to, 1:2] = inv * inv * total


def attention(raw, inv, ga, adv, cos, sin, start):
    rows, width = adv.shape[0], raw[0].shape[1]
    qw = ga[0].shape[1]
    half = rows // (2 * BLOCK) * BLOCK
    f32, bf16 = jnp.float32, jnp.bfloat16
    out_shape = [
        jax.ShapeDtypeStruct((half, width), bf16),
        jax.ShapeDtypeStruct((rows - half, width), bf16),
        jax.ShapeDtypeStruct((half, 2), f32),
        jax.ShapeDtypeStruct((rows - half, 2), f32),
        jax.ShapeDtypeStruct((rows, width), bf16),
        jax.ShapeDtypeStruct((rows, qw), bf16),
    ]
    operands = [*raw, *inv, *ga, adv, cos, sin, start]
    vmem = pl.BlockSpec(memory_space=pltpu.VMEM)
    return pl.pallas_call(
        attention_kernel,
        out_shape=out_shape,
        in_specs=[vmem] * len(operands),
        out_specs=[vmem] * len(out_shape),
        scratch_shapes=[
            pltpu.VMEM((rows + BLOCK, width), bf16),
            pltpu.VMEM((rows, qw), bf16),
            pltpu.VMEM((rows + BLOCK, HD), f32),
            pltpu.VMEM((rows + BLOCK, HD), f32),
        ],
        compiler_params=pltpu.CompilerParams(vmem_limit_bytes=14 * 1024 * 1024),
        cost_estimate=pl.CostEstimate(
            flops=rows * 2 * BLOCK * HD * 12 * (qw // HD),
            bytes_accessed=rows * width * 8 + rows * qw * 6,
            transcendentals=rows * 2 * BLOCK * (qw // HD),
        ),
        name="attention",
    )(*operands)


def project_kernel(count, feature_count, *refs):
    x_refs, w_refs = refs[:count], refs[count : 2 * count]
    raw_ref, square_ref = refs[-2:]
    raw, squares = None, None
    if len(refs) > 2 * count + 2:
        raw, squares = refs[2 * count][...], refs[2 * count + 1][...]
    for x_ref, w_ref in zip(x_refs, w_refs):
        part = matmul(x_ref[...], w_ref[...])
        raw = part if raw is None else raw + part
        wide = x_ref[...].astype(jnp.float32)
        part = jnp.sum(wide * wide, axis=1, keepdims=True)
        squares = part if squares is None else squares + part
    raw_ref[...] = raw
    if feature_count:
        squares = lax.rsqrt(squares / feature_count + NORM_EPSILON)
    square_ref[...] = squares


def project(parts, weights, prior, feature_count):
    rows, width = parts[0].shape[0], weights[0].shape[1]
    operands = [*parts, *weights, *prior]
    vmem = pl.BlockSpec(memory_space=pltpu.VMEM)
    return pl.pallas_call(
        functools.partial(project_kernel, len(parts), feature_count),
        out_shape=[
            jax.ShapeDtypeStruct((rows, width), jnp.float32),
            jax.ShapeDtypeStruct((rows, 1), jnp.float32),
        ],
        in_specs=[vmem] * len(operands),
        out_specs=[vmem] * 2,
        compiler_params=pltpu.CompilerParams(vmem_limit_bytes=12 * 1024 * 1024),
        cost_estimate=pl.CostEstimate(
            flops=2 * len(parts) * rows * width * parts[0].shape[1],
            bytes_accessed=2 * len(parts) * parts[0].shape[1] * (rows + width) + 8 * rows * width,
            transcendentals=rows,
        ),
        name="project",
    )(*operands)


def weight_grad_kernel(place_ref, *refs):
    heads, tails, g_tails = refs[:4], refs[4:8], refs[8:12]
    g_ref, scaled_ref, out_ref, gain_ref, term_ref = refs[12:]
    width = scaled_ref.shape[1]
    gain = gain_ref[0]
    gain = jnp.transpose(jnp.broadcast_to(gain, (HD, gain.shape[1])))[:, 0:1]
    first = g_ref.shape[0]
    for k in range(4):

        @pl.when(place_ref[pl.program_id(0)] == k)
        def _():
            total = contract_rows(heads[k][...], scaled_ref[:first, :])
            total += contract_rows(tails[k][...], scaled_ref[first:, :])
            term_ref[:, :width] = (total * gain).astype(jnp.bfloat16)
            total = contract_rows(g_ref[...], out_ref[:first, :])
            total += contract_rows(g_tails[k][...], out_ref[first:, :])
            term_ref[:, width:] = total.astype(jnp.bfloat16)


def weight_grads(places, heads, tails, g_tails, g_rows, scaled, out, gain):
    features = gain.shape[2]
    width = scaled.shape[1] + out.shape[1]
    vmem = pl.BlockSpec(memory_space=pltpu.VMEM)
    return pl.pallas_call(
        weight_grad_kernel,
        out_shape=jax.ShapeDtypeStruct((4 * features, width), jnp.bfloat16),
        grid_spec=pltpu.PrefetchScalarGridSpec(
            num_scalar_prefetch=1,
            grid=(4,),
            in_specs=[vmem] * 12
            + [pl.BlockSpec((g_rows.shape[0], features), lambda j, place: (0, j))]
            + [vmem] * 2
            + [pl.BlockSpec((1, 1, features), lambda j, place: (j, 0, 0))],
            out_specs=pl.BlockSpec((features, width), lambda j, place: (j, 0)),
        ),
        compiler_params=pltpu.CompilerParams(vmem_limit_bytes=40 * 1024 * 1024),
        cost_estimate=pl.CostEstimate(
            flops=2 * scaled.shape[0] * 4 * features * width,
            bytes_accessed=4 * features * (4 * scaled.shape[0] + 2 * width),
            transcendentals=0,
        ),
        name="weight_grads",
    )(places, *heads, *tails, *g_tails, g_rows, scaled, out, gain)


def per_device(roll_rows, dest, lengths, clusters, log_prob_grad, gain, w_q, w_k, w_v, w_o_t):
    sequence_count = dest.shape[0]
    max_len, local_features = roll_rows.shape[1:]
    row_count = log_prob_grad.shape[0]
    replicas = lax.axis_size("fsdp")
    per_pair = sequence_count // replicas
    me = lax.axis_index("fsdp")
    z = lax.axis_index("tp")
    f32, bf16 = jnp.float32, jnp.bfloat16
    q_cols, k_cols = w_q.shape[1], w_k.shape[1]
    qkv_cols = q_cols + 2 * k_cols
    feature_count = gain.shape[0]

    bounds = [0, row_count - 2 * BLOCK, row_count]
    g_rows = lax.all_gather(log_prob_grad[: bounds[1], :], "tp", axis=1, tiled=True)
    g_tail = log_prob_grad[bounds[1] :, :]
    g_near = gather_near(g_tail)
    g_far2 = gather_far(g_near, z)
    g_end = gather_end(g_far2)
    g_shards = shards(g_tail, g_near, g_far2, g_end, z)

    slot_ids = jnp.arange(sequence_count, dtype=jnp.int32)
    earlier_dest = dest[None, :] < dest[:, None]
    send_block = jnp.sum(earlier_dest.astype(jnp.int32), axis=1)
    source = jnp.sum(
        jnp.where(send_block[None, :] == slot_ids[:, None], slot_ids[None, :], 0), axis=1
    )
    send_rows = jnp.take(roll_rows, source, axis=0, mode="clip")
    arrived_rows = lax.all_to_all(send_rows, "fsdp", split_axis=0, concat_axis=0, tiled=True)

    ballots = clusters.reshape(sequence_count // GSIZE, GSIZE)
    vote_share = jnp.mean((ballots[:, :, None] == ballots[:, None, :]).astype(f32), axis=2)
    advantage = (vote_share - jnp.mean(vote_share, axis=1, keepdims=True)).reshape(sequence_count)
    tags = jnp.stack([(dest % sequence_count).astype(f32), advantage], axis=1)
    picked = send_block[None, :] == slot_ids[:, None]
    tags = jnp.sum(jnp.where(picked[:, :, None], tags[None, :, :], 0.0), axis=1).astype(bf16)
    tags = lax.all_to_all(tags, "fsdp", split_axis=0, concat_axis=0, tiled=True).astype(f32)
    holder = tags[None, :, 0].astype(jnp.int32) == slot_ids[:, None]
    slot_of = jnp.sum(jnp.where(holder, slot_ids[None, :], 0), axis=1)
    seq_advantage = jnp.sum(jnp.where(holder, tags[None, :, 1], 0.0), axis=1)

    lengths_row = lengths.reshape(sequence_count)
    sequence_ends = jnp.cumsum(lengths_row)
    sequence_starts = sequence_ends - lengths_row
    row_index = jnp.arange(row_count, dtype=jnp.int32)
    one_hot = (sequence_ends[None, :] > row_index[:, None]) & (
        sequence_starts[None, :] <= row_index[:, None]
    )
    row_start = jnp.sum(jnp.where(one_hot, sequence_starts[None, :], 0), axis=1)
    position = row_index - row_start
    row_slot = jnp.sum(jnp.where(one_hot, slot_of[None, :], 0), axis=1)
    adv = jnp.sum(jnp.where(one_hot, seq_advantage[None, :], 0.0), axis=1)[:, None]
    half_width = HD // 2
    frequency = ROPE_BASE ** (-(2.0 * jnp.arange(half_width, dtype=f32)) / HD)
    angles = position.astype(f32)[:, None] * frequency[None, :]
    cos, sin = jnp.cos(angles), jnp.sin(angles)
    cos = jnp.concatenate([cos, cos], axis=1)
    sin = jnp.concatenate([-sin, sin], axis=1)

    start = row_start[:, None]
    arrived_rows = after(arrived_rows, cos, sin, start, adv)
    x_own = jnp.take(
        arrived_rows.reshape(sequence_count * max_len, local_features),
        row_slot * max_len + position,
        axis=0,
        mode="clip",
    )
    x_head, x_tail = x_own[: bounds[1], :], x_own[bounds[1] :, :]
    tail_near = gather_near(x_tail)
    head_near = gather_near(after(x_head, tail_near[0], g_far2))
    tail_far2 = gather_far((after(tail_near[0], g_rows), tail_near[1]), z)
    head_far2 = gather_far((after(head_near[0], tail_far2), head_near[1]), z)

    w_qkv = lax.all_gather(
        jnp.concatenate([w_q, w_k, w_v], axis=1), "fsdp", axis=0, tiled=True
    )
    w_o = lax.all_gather(w_o_t, "fsdp", axis=0, tiled=True)
    gain_f = gain.astype(f32)
    gain_shards = gain_f.reshape(4, 1, local_features)
    w_shards = (w_qkv.astype(f32) * gain_f[:, None]).astype(bf16)
    w_shards = w_shards.reshape(4, local_features, qkv_cols)
    w_k_parts = [lax.dynamic_index_in_dim(w_shards, z ^ k, 0, keepdims=False) for k in range(4)]

    def input_terms(dqkv, scales, parts):
        return [
            (
                scales[:, 0:1] * times_trans(dqkv, w_k_parts[k])
                - parts[k].astype(f32) * (scales[:, 1:2] / feature_count)
            ).astype(bf16)
            for k in range(4)
        ]

    tail_end = gather_end(after(tail_far2, g_end, *head_near))
    tail_shards = shards(x_tail, tail_near, tail_far2, tail_end, z)
    raw1, inv1 = project(tail_shards, w_k_parts, (), feature_count)
    head_end = gather_end(after(head_far2, tail_end))
    w_o = after(w_o, head_far2)
    o_shards = w_o.reshape(4, local_features, q_cols)
    ga = [
        matmul(g_rows, w_o),
        sum(
            matmul(g_shards[k], lax.dynamic_index_in_dim(o_shards, z ^ k, 0, keepdims=False))
            for k in range(4)
        ),
    ]
    head_shards = shards(x_head, head_near, head_far2, after(head_end, raw1, *ga), z)
    raw0, inv0 = project(head_shards, w_k_parts, (), feature_count)
    dqkv0, dqkv1, scales0, scales1, scaled, out = attention(
        (raw0, raw1), (inv0, inv1), ga, adv, cos, sin, start
    )
    half = dqkv0.shape[0]
    terms0 = input_terms(dqkv0, scales0, [x[:half] for x in head_shards])
    end0 = scatter_end(terms0)
    total0 = far_total(terms0, end0)
    step0 = scatter_far(total0)
    dx0 = scatter_near(terms0, step0, z)

    places = jnp.stack([z ^ j for j in range(4)]).astype(jnp.int32)
    weight_terms = weight_grads(
        places,
        head_shards,
        tail_shards,
        g_shards,
        g_rows,
        after(scaled, terms0[3]),
        out,
        gain_shards,
    )
    summed = lax.psum_scatter(after(weight_terms, end0), "fsdp", scatter_dimension=0, tiled=True)

    terms1 = input_terms(
        after(dqkv1, end0),
        scales1,
        [jnp.concatenate([x[half:], y], axis=0) for x, y in zip(head_shards, tail_shards)],
    )
    end1 = scatter_end([*terms1[:3], after(terms1[3], end0)])
    step1 = scatter_far(far_total(terms1, after(end1, *step0)))
    dx1 = scatter_near(terms1, (after(step1[0], dx0), step1[1]), z)
    dx = jnp.concatenate([dx0, dx1], axis=0)
    input_grad = (adv * log_prob_grad.astype(f32) + dx).astype(bf16)
    grad_q = summed[:, :q_cols]
    grad_k = summed[:, q_cols : q_cols + k_cols]
    grad_v = summed[:, q_cols + k_cols : qkv_cols]
    grad_o_t = summed[:, qkv_cols:]
    return (input_grad, grad_q, grad_k, grad_v, grad_o_t)


def solution(mesh):
    in_specs = (
        P("fsdp", None, "tp"),
        P("fsdp"),
        P("fsdp", None),
        P("fsdp"),
        P("fsdp", "tp"),
        P(),
        P("fsdp", "tp"),
        P("fsdp", "tp"),
        P("fsdp", "tp"),
        P("fsdp", "tp"),
    )
    out_specs = (
        P("fsdp", "tp"),
        P("fsdp", "tp"),
        P("fsdp", "tp"),
        P("fsdp", "tp"),
        P("fsdp", "tp"),
    )
    return jax.shard_map(
        per_device, mesh=mesh, in_specs=in_specs, out_specs=out_specs, check_vma=False
    )
```

profile of v0, /device:TPU:0, one launch (start us, length us, event | category | flops | bytes accessed | tf_op | source)
XLA Modules:
  0.0 372.9 jit_solution(17530594766047055565)
XLA Ops:
  12.9 5.2 %all-to-all-start = ((bf16[8,4,2]{1,2,0:T(2,128)(2,1)}), bf16[8,4,2]{1,2,0:T(2,128)(2,1)S(1)}, u32[]{:S(2)}, u32[]{:S(2)}) async-start(bf16[8,4,2]{1,2,0:T(2,128)(2,1)} %copy.41), calls=%async_computation | async-start | bytes 8192 | tf_op jit(solution)/shard_map/all_to_all | solution.py:350
  18.2 5.7 %gather_fusion = bf16[32,72,896]{2,1,0:T(8,128)(2,1)} fusion(bf16[32,72,896]{2,1,0:T(8,128)(2,1)} %param.10, s32[1024]{0:T(1024)S(1)} %pad_clamp_fusion.1), kind=kCustom, calls=%fused_computation | custom fusion | bytes 8257664 | tf_op jit(solution)/shard_map/jit(_take)/gather | solution.py:341
  36.8 15.9 %collective-permute-done.1 = bf16[256,896]{1,0:T(8,128)(2,1)} collective-permute-done((bf16[256,896]{1,0:T(8,128)(2,1)S(1)}, bf16[256,896]{1,0:T(8,128)(2,1)}, u32[]{:S(2)}, u32[]{:S(2)}) %collective-permute-start.1) | collective-permute-done | bytes 458784 | tf_op jit(solution)/shard_map/ppermute | solution.py:45
  54.1 13.6 %collective-permute-done.3 = bf16[256,896]{1,0:T(8,128)(2,1)} collective-permute-done((bf16[256,896]{1,0:T(8,128)(2,1)S(1)}, bf16[256,896]{1,0:T(8,128)(2,1)}, u32[]{:S(2)}, u32[]{:S(2)}) %collective-permute-start.3) | collective-permute-done | bytes 458784 | tf_op jit(solution)/shard_map/ppermute | solution.py:45
  71.0 6.0 %all-to-all-done.1 = bf16[32,72,896]{2,1,0:T(8,128)(2,1)} async-done(((bf16[32,72,896]{2,1,0:T(8,128)(2,1)}), bf16[32,72,896]{2,1,0:T(8,128)(2,1)}, u32[]{:S(2)}, u32[]{:S(2)}) %all-to-all-start.1) | async-done | bytes 4128800 | tf_op jit(solution)/shard_map/all_to_all | solution.py:342
  77.0 6.2 %gather_fusion.1 = bf16[768,896]{1,0:T(8,128)(2,1)S(1)} fusion(bf16[2304,896]{1,0:T(8,128)(2,1)} %bitcast.5, s32[1024]{0:T(1024)S(1)} %pad_clamp_fusion), kind=kCustom, calls=%fused_computation.1 | custom fusion | bytes 2755584 | tf_op jit(solution)/shard_map/jit(_take)/gather | solution.py:375
  87.6 12.1 %collective-permute-done.4 = bf16[256,896]{1,0:T(8,128)(2,1)} collective-permute-done((bf16[256,896]{1,0:T(8,128)(2,1)}, bf16[256,896]{1,0:T(8,128)(2,1)}, u32[]{:S(2)}, u32[]{:S(2)}) %collective-permute-start.4) | collective-permute-done | bytes 458784 | tf_op jit(solution)/shard_map/ppermute | solution.py:50
  103.9 12.1 %collective-permute-start.5 = (bf16[512,896]{1,0:T(8,128)(2,1)S(1)}, bf16[512,896]{1,0:T(8,128)(2,1)}, u32[]{:S(2)}, u32[]{:S(2)}) collective-permute-start(bf16[512,896]{1,0:T(8,128)(2,1)S(1)} %slice.104.refs_0_), channel_id=1, source_target_pairs={{0,1},{1,2},{2,3},{4,5},{5,6},{6,7},{8,9},{9,10},{10,11},{12,13},{... | collective-permute-start | bytes 2752520 | tf_op jit(solution)/shard_map/ppermute | solution.py:45
  122.4 16.3 %collective-permute-done.6 = bf16[512,896]{1,0:T(8,128)(2,1)} collective-permute-done((bf16[512,896]{1,0:T(8,128)(2,1)S(1)}, bf16[512,896]{1,0:T(8,128)(2,1)}, u32[]{:S(2)}, u32[]{:S(2)}) %collective-permute-start.6) | collective-permute-done | bytes 917536 | tf_op jit(solution)/shard_map/ppermute | solution.py:45
  140.0 8.4 %collective-permute-done.9 = bf16[256,896]{1,0:T(8,128)(2,1)S(1)} collective-permute-done((bf16[256,896]{1,0:T(8,128)(2,1)}, bf16[256,896]{1,0:T(8,128)(2,1)S(1)}, u32[]{:S(2)}, u32[]{:S(2)}) %collective-permute-start.9) | collective-permute-done | bytes 458784 | tf_op jit(solution)/shard_map/ppermute | solution.py:50
  151.9 6.3 %collective-permute-done.12 = bf16[256,896]{1,0:T(8,128)(2,1)S(1)} collective-permute-done((bf16[256,896]{1,0:T(8,128)(2,1)S(1)}, bf16[256,896]{1,0:T(8,128)(2,1)S(1)}, u32[]{:S(2)}, u32[]{:S(2)}) %collective-permute-start.12) | collective-permute-done | bytes 458784 | tf_op jit(solution)/shard_map/ppermute | solution.py:55
  163.8 21.6 %collective-permute-done.13 = bf16[256,896]{1,0:T(8,128)(2,1)} collective-permute-done((bf16[256,896]{1,0:T(8,128)(2,1)S(1)}, bf16[256,896]{1,0:T(8,128)(2,1)}, u32[]{:S(2)}, u32[]{:S(2)}) %collective-permute-start.13) | collective-permute-done | bytes 458784 | tf_op jit(solution)/shard_map/ppermute | solution.py:55
  207.0 5.0 %collective-permute-done.14 = bf16[512,896]{1,0:T(8,128)(2,1)} collective-permute-done((bf16[512,896]{1,0:T(8,128)(2,1)}, bf16[512,896]{1,0:T(8,128)(2,1)}, u32[]{:S(2)}, u32[]{:S(2)}) %collective-permute-start.14) | collective-permute-done | bytes 917536 | tf_op jit(solution)/shard_map/ppermute | solution.py:55
  214.1 5.6 %project.3 = (f32[512,768]{1,0:T(8,128)S(1)}, f32[512,1]{1,0:T(8,128)S(1)}) custom-call(bf16[512,896]{1,0:T(8,128)(2,1)S(1)} %copy-done.29, bf16[512,896]{1,0:T(8,128)(2,1)S(1)} %get-tuple-element.64.refs_1_, bf16[512,896]{1,0:T(8,128)(2,1)} %broadcast_select_fusion.refs_2_, bf16[512,896]{1,0:T(8,128)(2,1)S(1)} %get-tuple-element.63.refs_3_, ...), custom_call_target="tpu_custom_call" | custom-call | flops 2818572288 | bytes 12320768 | tf_op jit(solution)/shard_map/project/pallas_call | solution.py:251
  219.8 21.4 %attention.1 = (bf16[384,768]{1,0:T(8,128)(2,1)S(1)}, bf16[384,768]{1,0:T(8,128)(2,1)S(1)}, f32[384,2]{1,0:T(8,128)S(1)}, f32[384,2]{1,0:T(8,128)S(1)}, bf16[768...) custom-call(f32[512,768]{1,0:T(8,128)S(1)} %get-tuple-element.38.refs_0_, f32[256,768]{1,0:T(8,128)S(1)} %get-tuple-element.35.refs_1_, ...), custom_call_target="tpu_custom_call" | custom-call | flops 1207959552 | bytes 7077888 | tf_op jit(solution)/shard_map/attention/pallas_call | solution.py:208
  260.7 12.4 %weight_grads.1 = bf16[3584,1280]{1,0:T(8,128)(2,1)} custom-call(s32[4]{0:T(128)S(1)} %pad_add_fusion.place_ref, bf16[512,896]{1,0:T(8,128)(2,1)S(1)} %copy-done.30, bf16[512,896]{1,0:T(8,128)(2,1)S(1)} %copy-done.23, bf16[512,896]{1,0:T(8,128)(2,1)} %broadcast_select_fusion.refs_2_, bf16[512,896]{1,0:T(8,128)(2,1)S(1)} %copy-done.26, ...), custom_call_target="tpu_custom_call" | custom-call | flops 7046430720 | bytes 20185088 | tf_op jit(solution)/shard_map/weight_grads/pallas_call | solution.py:292
  284.4 9.8 %collective-permute-done.20 = bf16[384,896]{1,0:T(8,128)(2,1)S(1)} collective-permute-done((bf16[384,896]{1,0:T(8,128)(2,1)S(1)}, bf16[384,896]{1,0:T(8,128)(2,1)S(1)}, u32[]{:S(2)}, u32[]{:S(2)}) %collective-permute-start.20) | collective-permute-done | bytes 688160 | tf_op jit(solution)/shard_map/ppermute | solution.py:70
  294.2 10.5 %collective-permute-done.16 = bf16[384,896]{1,0:T(8,128)(2,1)S(1)} collective-permute-done((bf16[384,896]{1,0:T(8,128)(2,1)S(1)}, bf16[384,896]{1,0:T(8,128)(2,1)S(1)}, u32[]{:S(2)}, u32[]{:S(2)}) %collective-permute-start.16) | collective-permute-done | bytes 688160 | tf_op jit(solution)/shard_map/ppermute | solution.py:78
  308.2 5.2 %collective-permute-start.17 = (bf16[384,896]{1,0:T(8,128)(2,1)S(1)}, bf16[384,896]{1,0:T(8,128)(2,1)S(1)}, u32[]{:S(2)}, u32[]{:S(2)}) collective-permute-start(bf16[384,896]{1,0:T(8,128)(2,1)S(1)} %get-tuple-element.67), channel_id=1, source_target_pairs={{0,1},{1,2},{2,3},{4,5},{5,6},{6,7},{8,9},{9,10},{10,11},{12,13},{... | collective-permute-start | bytes 2064392 | tf_op jit(solution)/shard_map/ppermute | solution.py:87
  313.8 7.6 %collective-permute-start.21 = (bf16[384,896]{1,0:T(8,128)(2,1)S(1)}, bf16[384,896]{1,0:T(8,128)(2,1)S(1)}, u32[]{:S(2)}, u32[]{:S(2)}) collective-permute-start(bf16[384,896]{1,0:T(8,128)(2,1)S(1)} %add_convert_fusion.2), channel_id=1, source_target_pairs={{0,1},{1,2},{4,5},{5,6},{8,9},{9,10},{12,13},{13,14},{16,17},{17,1... | collective-permute-start | bytes 2064392 | tf_op jit(solution)/shard_map/ppermute | solution.py:78
  324.0 5.2 %collective-permute-done.17 = bf16[384,896]{1,0:T(8,128)(2,1)S(1)} collective-permute-done((bf16[384,896]{1,0:T(8,128)(2,1)S(1)}, bf16[384,896]{1,0:T(8,128)(2,1)S(1)}, u32[]{:S(2)}, u32[]{:S(2)}) %collective-permute-start.17) | collective-permute-done | bytes 688160 | tf_op jit(solution)/shard_map/ppermute | solution.py:87
  329.5 9.4 %collective-permute-done.21 = bf16[384,896]{1,0:T(8,128)(2,1)S(1)} collective-permute-done((bf16[384,896]{1,0:T(8,128)(2,1)S(1)}, bf16[384,896]{1,0:T(8,128)(2,1)S(1)}, u32[]{:S(2)}, u32[]{:S(2)}) %collective-permute-start.21) | collective-permute-done | bytes 688160 | tf_op jit(solution)/shard_map/ppermute | solution.py:78
  340.6 9.1 %collective-permute-start.22 = (bf16[384,896]{1,0:T(8,128)(2,1)S(1)}, bf16[384,896]{1,0:T(8,128)(2,1)S(1)}, u32[]{:S(2)}, u32[]{:S(2)}) collective-permute-start(bf16[384,896]{1,0:T(8,128)(2,1)S(1)} %get-tuple-element.65), channel_id=1, source_target_pairs={{0,1},{1,2},{2,3},{4,5},{5,6},{6,7},{8,9},{9,10},{10,11},{12,13},{... | collective-permute-start | bytes 2064392 | tf_op jit(solution)/shard_map/ppermute | solution.py:87
  350.6 8.8 %collective-permute-done.24 = bf16[384,896]{1,0:T(8,128)(2,1)S(1)} collective-permute-done((bf16[384,896]{1,0:T(8,128)(2,1)S(1)}, bf16[384,896]{1,0:T(8,128)(2,1)S(1)}, u32[]{:S(2)}, u32[]{:S(2)}) %collective-permute-start.24) | collective-permute-done | bytes 688160 | tf_op jit(solution)/shard_map/ppermute | solution.py:88
  (243 shorter events, 118.2 us)
Async XLA Ops:
  7.2 113.2 %all-gather.4.cloned.1.call-start = ((), (), s32[]{:S(2)}) async-start(), calls=%async_computation.3 | async-start | bytes 4587520 | tf_op jit(solution)/shard_map/all_gather | solution.py:328
  9.6 181.9 %all-gather.8.cloned.1.call-start = ((), (), s32[]{:S(2)}) async-start(), calls=%async_computation.5 | async-start | bytes 4128768 | tf_op jit(solution)/shard_map/all_gather | solution.py:390
  10.3 189.9 %all-gather.6.cloned.1.call-start = ((), (), s32[]{:S(2)}) async-start(), calls=%async_computation.4 | async-start | bytes 6193152 | tf_op jit(solution)/shard_map/all_gather | solution.py:387
  23.9 53.1 %all-to-all-start.1 = ((bf16[32,72,896]{2,1,0:T(8,128)(2,1)}), bf16[32,72,896]{2,1,0:T(8,128)(2,1)}, u32[]{:S(2)}, u32[]{:S(2)}) async-start(bf16[32,72,896]{2,1,0:T(8,128)(2,1)} %gather_fusion), calls=%async_computation.1 | async-start | bytes 8257536 | tf_op jit(solution)/shard_map/all_to_all | solution.py:342
  28.6 333.8 %reduce-scatter.2.cloned.1.call-start = ((), (), s32[]{:S(2)}) async-start(), calls=%async_computation.6 | async-start | bytes 10321920 | tf_op jit(solution)/shard_map/reduce_scatter | solution.py:442
  28.7 24.0 %collective-permute-start.1 = (bf16[256,896]{1,0:T(8,128)(2,1)S(1)}, bf16[256,896]{1,0:T(8,128)(2,1)}, u32[]{:S(2)}, u32[]{:S(2)}) collective-permute-start(bf16[256,896]{1,0:T(8,128)(2,1)S(1)} %slice.83.refs_8_), channel_id=1, source_target_pairs={{0,1},{1,2},{2,3},{4,5},{5,6},{6,7},{8,9},{9,10},{10,11},{12,13},{... | collective-permute-start | bytes 1376264 | tf_op jit(solution)/shard_map/ppermute | solution.py:45
  33.0 34.8 %collective-permute-start.3 = (bf16[256,896]{1,0:T(8,128)(2,1)S(1)}, bf16[256,896]{1,0:T(8,128)(2,1)}, u32[]{:S(2)}, u32[]{:S(2)}) collective-permute-start(bf16[256,896]{1,0:T(8,128)(2,1)S(1)} %slice.83.refs_8_), channel_id=1, source_target_pairs={{1,0},{2,1},{3,2},{5,4},{6,5},{7,6},{9,8},{10,9},{11,10},{13,12},{... | collective-permute-start | bytes 1376264 | tf_op jit(solution)/shard_map/ppermute | solution.py:45
  52.7 34.9 %collective-permute-start.2 = (bf16[256,896]{1,0:T(8,128)(2,1)}, bf16[256,896]{1,0:T(8,128)(2,1)}, u32[]{:S(2)}, u32[]{:S(2)}) collective-permute-start(bf16[256,896]{1,0:T(8,128)(2,1)} %collective-permute-done.1), channel_id=1, source_target_pairs={{1,2},{2,3},{5,6},{6,7},{9,10},{10,11},{13,14},{14,15},{17,18},{18... | collective-permute-start | bytes 1376264 | tf_op jit(solution)/shard_map/ppermute | solution.py:49
  67.8 31.9 %collective-permute-start.4 = (bf16[256,896]{1,0:T(8,128)(2,1)}, bf16[256,896]{1,0:T(8,128)(2,1)}, u32[]{:S(2)}, u32[]{:S(2)}) collective-permute-start(bf16[256,896]{1,0:T(8,128)(2,1)} %collective-permute-done.3), channel_id=1, source_target_pairs={{1,0},{2,1},{5,4},{6,5},{9,8},{10,9},{13,12},{14,13},{17,16},{18,1... | collective-permute-start | bytes 1376264 | tf_op jit(solution)/shard_map/ppermute | solution.py:50
  102.6 36.1 %collective-permute-start.6 = (bf16[512,896]{1,0:T(8,128)(2,1)S(1)}, bf16[512,896]{1,0:T(8,128)(2,1)}, u32[]{:S(2)}, u32[]{:S(2)}) collective-permute-start(bf16[512,896]{1,0:T(8,128)(2,1)S(1)} %slice.104.refs_0_), channel_id=1, source_target_pairs={{1,0},{2,1},{3,2},{5,4},{6,5},{7,6},{9,8},{10,9},{11,10},{13,12},{... | collective-permute-start | bytes 2752520 | tf_op jit(solution)/shard_map/ppermute | solution.py:45
  103.9 46.4 %collective-permute-start.5 = (bf16[512,896]{1,0:T(8,128)(2,1)S(1)}, bf16[512,896]{1,0:T(8,128)(2,1)}, u32[]{:S(2)}, u32[]{:S(2)}) collective-permute-start(bf16[512,896]{1,0:T(8,128)(2,1)S(1)} %slice.104.refs_0_), channel_id=1, source_target_pairs={{0,1},{1,2},{2,3},{4,5},{5,6},{6,7},{8,9},{9,10},{10,11},{12,13},{... | collective-permute-start | bytes 2752520 | tf_op jit(solution)/shard_map/ppermute | solution.py:45
  119.0 29.4 %collective-permute-start.9 = (bf16[256,896]{1,0:T(8,128)(2,1)}, bf16[256,896]{1,0:T(8,128)(2,1)S(1)}, u32[]{:S(2)}, u32[]{:S(2)}) collective-permute-start(bf16[256,896]{1,0:T(8,128)(2,1)} %collective-permute-done.8), channel_id=1, source_target_pairs={{1,0},{2,1},{5,4},{6,5},{9,8},{10,9},{13,12},{14,13},{17,16},{18,1... | collective-permute-start | bytes 1376264 | tf_op jit(solution)/shard_map/ppermute | solution.py:50
  120.4 28.8 %collective-permute-start.7 = (bf16[256,896]{1,0:T(8,128)(2,1)}, bf16[256,896]{1,0:T(8,128)(2,1)S(1)}, u32[]{:S(2)}, u32[]{:S(2)}) collective-permute-start(bf16[256,896]{1,0:T(8,128)(2,1)} %collective-permute-done), channel_id=1, source_target_pairs={{1,2},{2,3},{5,6},{6,7},{9,10},{10,11},{13,14},{14,15},{17,18},{18... | collective-permute-start | bytes 1376264 | tf_op jit(solution)/shard_map/ppermute | solution.py:49
  121.1 37.2 %collective-permute-start.12 = (bf16[256,896]{1,0:T(8,128)(2,1)S(1)}, bf16[256,896]{1,0:T(8,128)(2,1)S(1)}, u32[]{:S(2)}, u32[]{:S(2)}) collective-permute-start(bf16[256,896]{1,0:T(8,128)(2,1)S(1)} %broadcast_select_fusion.5.refs_10_), channel_id=1, source_target_pairs={{2,3},{1,0},{6,7},{5,4},{10,11},{9,8},{14,15},{13,12},{18,19},{17,... | collective-permute-start | bytes 1376264 | tf_op jit(solution)/shard_map/ppermute | solution.py:55
  138.7 49.0 %collective-permute-start.11 = (bf16[512,896]{1,0:T(8,128)(2,1)}, bf16[512,896]{1,0:T(8,128)(2,1)}, u32[]{:S(2)}, u32[]{:S(2)}) collective-permute-start(bf16[512,896]{1,0:T(8,128)(2,1)} %collective-permute-done.6), channel_id=1, source_target_pairs={{1,0},{2,1},{5,4},{6,5},{9,8},{10,9},{13,12},{14,13},{17,16},{18,1... | collective-permute-start | bytes 2752520 | tf_op jit(solution)/shard_map/ppermute | solution.py:50
  150.3 37.3 %collective-permute-start.10 = (bf16[512,896]{1,0:T(8,128)(2,1)}, bf16[512,896]{1,0:T(8,128)(2,1)}, u32[]{:S(2)}, u32[]{:S(2)}) collective-permute-start(bf16[512,896]{1,0:T(8,128)(2,1)} %collective-permute-done.5), channel_id=1, source_target_pairs={{1,2},{2,3},{5,6},{6,7},{9,10},{10,11},{13,14},{14,15},{17,18},{18... | collective-permute-start | bytes 2752520 | tf_op jit(solution)/shard_map/ppermute | solution.py:49
  159.0 26.3 %collective-permute-start.13 = (bf16[256,896]{1,0:T(8,128)(2,1)S(1)}, bf16[256,896]{1,0:T(8,128)(2,1)}, u32[]{:S(2)}, u32[]{:S(2)}) collective-permute-start(bf16[256,896]{1,0:T(8,128)(2,1)S(1)} %broadcast_select_fusion.4.refs_2_.refs_6_), channel_id=1, source_target_pairs={{2,3},{1,0},{6,7},{5,4},{10,11},{9,8},{14,15},{13,12},{18,19},{17,... | collective-permute-start | bytes 1376264 | tf_op jit(solution)/shard_map/ppermute | solution.py:55
  189.9 22.1 %collective-permute-start.14 = (bf16[512,896]{1,0:T(8,128)(2,1)}, bf16[512,896]{1,0:T(8,128)(2,1)}, u32[]{:S(2)}, u32[]{:S(2)}) collective-permute-start(bf16[512,896]{1,0:T(8,128)(2,1)} %broadcast_select_fusion.refs_2_), channel_id=1, source_target_pairs={{2,3},{1,0},{6,7},{5,4},{10,11},{9,8},{14,15},{13,12},{18,19},{17,... | collective-permute-start | bytes 2752520 | tf_op jit(solution)/shard_map/ppermute | solution.py:55
  243.2 30.0 %collective-permute-start.15 = (bf16[384,896]{1,0:T(8,128)(2,1)}, bf16[384,896]{1,0:T(8,128)(2,1)}, u32[]{:S(2)}, u32[]{:S(2)}) collective-permute-start(bf16[384,896]{1,0:T(8,128)(2,1)} %subtract_convert_fusion.3), channel_id=1, source_target_pairs={{3,2},{0,1},{7,6},{4,5},{11,10},{8,9},{15,14},{12,13},{19,18},{16,... | collective-permute-start | bytes 2064392 | tf_op jit(solution)/shard_map/ppermute | solution.py:70
  280.6 24.2 %collective-permute-start.16 = (bf16[384,896]{1,0:T(8,128)(2,1)S(1)}, bf16[384,896]{1,0:T(8,128)(2,1)S(1)}, u32[]{:S(2)}, u32[]{:S(2)}) collective-permute-start(bf16[384,896]{1,0:T(8,128)(2,1)S(1)} %add_convert_fusion.5), channel_id=1, source_target_pairs={{0,1},{1,2},{4,5},{5,6},{8,9},{9,10},{12,13},{13,14},{16,17},{17,1... | collective-permute-start | bytes 2064392 | tf_op jit(solution)/shard_map/ppermute | solution.py:78
  281.9 22.8 %collective-permute-start.18 = (bf16[384,896]{1,0:T(8,128)(2,1)S(1)}, bf16[384,896]{1,0:T(8,128)(2,1)S(1)}, u32[]{:S(2)}, u32[]{:S(2)}) collective-permute-start(bf16[384,896]{1,0:T(8,128)(2,1)S(1)} %add_convert_fusion.5), channel_id=1, source_target_pairs={{3,2},{2,1},{7,6},{6,5},{11,10},{10,9},{15,14},{14,13},{19,18},{18... | collective-permute-start | bytes 2064392 | tf_op jit(solution)/shard_map/ppermute | solution.py:78
  308.2 21.0 %collective-permute-start.17 = (bf16[384,896]{1,0:T(8,128)(2,1)S(1)}, bf16[384,896]{1,0:T(8,128)(2,1)S(1)}, u32[]{:S(2)}, u32[]{:S(2)}) collective-permute-start(bf16[384,896]{1,0:T(8,128)(2,1)S(1)} %get-tuple-element.67), channel_id=1, source_target_pairs={{0,1},{1,2},{2,3},{4,5},{5,6},{6,7},{8,9},{9,10},{10,11},{12,13},{... | collective-permute-start | bytes 2064392 | tf_op jit(solution)/shard_map/ppermute | solution.py:87
  313.8 25.1 %collective-permute-start.21 = (bf16[384,896]{1,0:T(8,128)(2,1)S(1)}, bf16[384,896]{1,0:T(8,128)(2,1)S(1)}, u32[]{:S(2)}, u32[]{:S(2)}) collective-permute-start(bf16[384,896]{1,0:T(8,128)(2,1)S(1)} %add_convert_fusion.2), channel_id=1, source_target_pairs={{0,1},{1,2},{4,5},{5,6},{8,9},{9,10},{12,13},{13,14},{16,17},{17,1... | collective-permute-start | bytes 2064392 | tf_op jit(solution)/shard_map/ppermute | solution.py:78
  339.3 20.1 %collective-permute-start.24 = (bf16[384,896]{1,0:T(8,128)(2,1)S(1)}, bf16[384,896]{1,0:T(8,128)(2,1)S(1)}, u32[]{:S(2)}, u32[]{:S(2)}) collective-permute-start(bf16[384,896]{1,0:T(8,128)(2,1)S(1)} %get-tuple-element.66), channel_id=1, source_target_pairs={{1,0},{2,1},{3,2},{5,4},{6,5},{7,6},{9,8},{10,9},{11,10},{13,12},{... | collective-permute-start | bytes 2064392 | tf_op jit(solution)/shard_map/ppermute | solution.py:88
  (65 other events, 726.0 us)
Sparse Core Ops, SparseCore 0:
  9.7 94.1 all-gather.3
  105.7 34.4 all-gather.7
  142.1 42.2 all-gather.5
  273.3 78.3 reduce-scatter.1
where the time goes:
time: 376 us; the launch traced here: 373 us
  waiting for transfers between devices  154 us (41%)
  starting transfers between devices  77.5 us (21%)
  local copies, waits for them, and re-layouts  42.1 us (11%)
  Pallas kernels  41.3 us (11%)
  other arithmetic  22.8 us (6%)
  matrix products  20 us (5%)
  between operations  15.1 us (4%)
    ppermute x6, waiting for transfers between devices, gather_near(): return (lax.ppermute(own, 'tp', UP), lax.ppermute(own, 'tp', DOWN))  49 us
    ppermute x3, waiting for transfers between devices, gather_end(): return lax.ppermute(far2, 'tp', TO_ENDS)  33 us
    ppermute x6, starting transfers between devices, gather_near(): return (lax.ppermute(own, 'tp', UP), lax.ppermute(own, 'tp', DOWN))  24.5 us
    pallas_call x1, Pallas kernels, attention(): pl.pallas_call(attention_kernel, out_shape=out_shape, in_specs=[vmem] * l...  21.4 us
    ppermute x3, waiting for transfers between devices, gather_far(): down2 = lax.ppermute(step1[1], 'tp', DOWN_MID)  20.6 us
    ppermute x2, waiting for transfers between devices, scatter_far(): lax.ppermute(total2, 'tp', UP_IN)  19.9 us
    unnamed x116, local copies, waits for them, and re-layouts  18.5 us
    ppermute x2, starting transfers between devices, scatter_near(): up3 = lax.ppermute(go_up.astype(jnp.bfloat16), 'tp', UP)  14.3 us
  transfers between devices with their start and end apart: 31, of which 16 were waited for; matrix products, arithmetic and copies ran while one was open for 15% of the time, Pallas kernels for 4%

commit v1 on v0

--- a/solution.py
+++ b/solution.py
@@ -92,58 +92,45 @@
 def attention_kernel(*refs):
     raw_refs, inv_refs, ga_refs = refs[:2], refs[2:4], refs[4:6]
     adv_ref, cos_ref, sin_ref, start_ref = refs[6:10]
-    dqkv_refs, scale_refs = refs[10:12], refs[12:14]
-    dscaled_ref, out_ref, qkv_b, dq_b, dk_acc, dv_acc = refs[14:]
+    dqkv_ref, scale_ref, dscaled_ref, out_ref, qkv_b, dk_acc, dv_acc = refs[10:]
     heads = ga_refs[0].shape[1] // HD
     qw = heads * HD
     scale = HD ** (-0.5)
     f32, bf16 = jnp.float32, jnp.bfloat16
-    blocks = adv_ref.shape[0] // BLOCK
-
-    def span(block):
-        return slice(block * BLOCK, (block + 1) * BLOCK)
-
-    def piece(pair, block):
-        first = pair[0].shape[0] // BLOCK
-        return (pair[0], span(block)) if block < first else (pair[1], span(block - first))
-
-    def read(pair, block, cols):
-        ref, rows = piece(pair, block)
-        return ref[rows, cols]
+    pieces = list(zip(raw_refs, inv_refs, ga_refs, (0, raw_refs[0].shape[0])))
+    edge = pl.ds(0, BLOCK)
+    qkv_b[edge, :] = jnp.zeros((BLOCK, qkv_b.shape[1]), bf16)
+    dk_acc[edge, :] = jnp.zeros((BLOCK, HD), f32)
+    dv_acc[edge, :] = jnp.zeros((BLOCK, HD), f32)
 
     def turn(value, cos, sin):
         return value * cos + pltpu.roll(value, HD // 2, 1) * sin
 
-    def inverse(block):
-        return read(inv_refs, block, slice(0, 1))
-
-    qkv_b[span(0), :] = jnp.zeros((BLOCK, qkv_b.shape[1]), bf16)
-    dk_acc[span(0), :] = jnp.zeros((BLOCK, HD), f32)
-    dv_acc[span(0), :] = jnp.zeros((BLOCK, HD), f32)
-
-    for block in range(blocks):
-        here, after = span(block), span(block + 1)
-        both = slice(block * BLOCK, (block + 2) * BLOCK)
+    def rows_of(block, first):
+        base = pl.multiple_of(block * BLOCK, BLOCK)
+        return base + first, pl.ds(base, BLOCK), pl.ds(base + first, BLOCK)
+
+    def forward_and_back(raw_ref, inv_ref, ga_ref, first, block, carry):
+        base, local, here = rows_of(block, first)
+        after = pl.ds(base + BLOCK, BLOCK)
+        both = pl.ds(base, 2 * BLOCK)
         cos, sin = cos_ref[here, :], sin_ref[here, :]
-        inv = inverse(block)
+        inv = inv_ref[local, :]
         for h in range(heads + 2):
             cols = slice(h * HD, (h + 1) * HD)
-            linear = read(raw_refs, block, cols) * inv
+            linear = raw_ref[local, cols] * inv
             qkv_b[after, cols] = (turn(linear, cos, sin) if h <= heads else linear).astype(bf16)
         adv = adv_ref[here, :]
         qs = jnp.concatenate(
             [qkv_b[after, h * HD : (h + 1) * HD] for h in range(heads)], axis=0
         )
         gs = jnp.concatenate(
-            [
-                (read(ga_refs, block, slice(h * HD, (h + 1) * HD)) * adv).astype(bf16)
-                for h in range(heads)
-            ],
+            [(ga_ref[local, h * HD : (h + 1) * HD] * adv).astype(bf16) for h in range(heads)],
             axis=0,
         )
         ks = qkv_b[both, qw : qw + HD]
         vs = qkv_b[both, qw + HD : qw + 2 * HD]
-        start = start_ref[here, :] - (block - 1) * BLOCK
+        start = start_ref[here, :] - (base - BLOCK)
         col = lax.broadcasted_iota(jnp.int32, (BLOCK, 2 * BLOCK), 1)
         row = lax.broadcasted_iota(jnp.int32, (BLOCK, 2 * BLOCK), 0) + BLOCK
         bias = jnp.where((col >= start) & (col <= row), 0.0, -1e30)
@@ -164,42 +151,45 @@
         dv_acc[after, :] = contract_rows(prob_b[:, BLOCK:], gs)
         for h in range(heads):
             cols = slice(h * HD, (h + 1) * HD)
-            out_ref[here, cols] = (out[span(h), :].astype(bf16).astype(f32) * adv).astype(bf16)
-            dq_b[here, cols] = turn(dq[span(h), :], cos, -sin).astype(bf16)
-
-    for block in range(blocks):
-        here, after = span(block), span(block + 1)
-        cos, sin = cos_ref[here, :], sin_ref[here, :]
-        inv = inverse(block)
-        dqkv_ref, to = piece(dqkv_refs, block)
+            part = slice(h * BLOCK, (h + 1) * BLOCK)
+            out_ref[here, cols] = (out[part, :].astype(bf16).astype(f32) * adv).astype(bf16)
+            dqkv_ref[here, cols] = turn(dq[part, :], cos, -sin).astype(bf16)
+        return carry
+
+    def finish(raw_ref, inv_ref, ga_ref, first, block, carry):
+        base, local, here = rows_of(block, first)
+        after = pl.ds(base + BLOCK, BLOCK)
+        inv = inv_ref[local, :]
         total = jnp.zeros((BLOCK, 1), f32)
         for h in range(heads + 2):
             cols = slice(h * HD, (h + 1) * HD)
             if h < heads:
-                grad = dq_b[here, cols]
+                grad = dqkv_ref[here, cols]
             elif h == heads:
-                grad = turn(dk_acc[after, :], cos, -sin).astype(bf16)
+                grad = turn(dk_acc[after, :], cos_ref[here, :], -sin_ref[here, :]).astype(bf16)
+                dqkv_ref[here, cols] = grad
             else:
                 grad = dv_acc[after, :].astype(bf16)
-            dqkv_ref[to, cols] = grad
+                dqkv_ref[here, cols] = grad
             grad = grad.astype(f32) * inv
             dscaled_ref[here, cols] = grad.astype(bf16)
-            total += jnp.sum(grad * read(raw_refs, block, cols), axis=-1, keepdims=True)
-        scale_ref, to = piece(scale_refs, block)
-        scale_ref[to, 0:1] = inv
-        scale_ref[to, 1:2] = inv * inv * total
+            total += jnp.sum(grad * raw_ref[local, cols], axis=-1, keepdims=True)
+        scale_ref[here, 0:1] = inv
+        scale_ref[here, 1:2] = inv * inv * total
+        return carry
+
+    for body in (forward_and_back, finish):
+        for piece in pieces:
+            lax.fori_loop(0, piece[0].shape[0] // BLOCK, functools.partial(body, *piece), 0)
 
 
 def attention(raw, inv, ga, adv, cos, sin, start):
     rows, width = adv.shape[0], raw[0].shape[1]
     qw = ga[0].shape[1]
-    half = rows // (2 * BLOCK) * BLOCK
     f32, bf16 = jnp.float32, jnp.bfloat16
     out_shape = [
-        jax.ShapeDtypeStruct((half, width), bf16),
-        jax.ShapeDtypeStruct((rows - half, width), bf16),
-        jax.ShapeDtypeStruct((half, 2), f32),
-        jax.ShapeDtypeStruct((rows - half, 2), f32),
+        jax.ShapeDtypeStruct((rows, width), bf16),
+        jax.ShapeDtypeStruct((rows, 2), f32),
         jax.ShapeDtypeStruct((rows, width), bf16),
         jax.ShapeDtypeStruct((rows, qw), bf16),
     ]
@@ -212,7 +202,6 @@
         out_specs=[vmem] * len(out_shape),
         scratch_shapes=[
             pltpu.VMEM((rows + BLOCK, width), bf16),
-            pltpu.VMEM((rows, qw), bf16),
             pltpu.VMEM((rows + BLOCK, HD), f32),
             pltpu.VMEM((rows + BLOCK, HD), f32),
         ],
@@ -288,16 +277,20 @@
 def weight_grads(places, heads, tails, g_tails, g_rows, scaled, out, gain):
     features = gain.shape[2]
     width = scaled.shape[1] + out.shape[1]
-    vmem = pl.BlockSpec(memory_space=pltpu.VMEM)
+    x_parts = [*heads, *tails, *g_tails]
+
+    def once(o):
+        return pl.BlockSpec(o.shape, lambda j, place: (0, 0), pipeline_mode=pl.Buffered(1))
+
     return pl.pallas_call(
         weight_grad_kernel,
         out_shape=jax.ShapeDtypeStruct((4 * features, width), jnp.bfloat16),
         grid_spec=pltpu.PrefetchScalarGridSpec(
             num_scalar_prefetch=1,
             grid=(4,),
-            in_specs=[vmem] * 12
+            in_specs=[once(o) for o in x_parts]
             + [pl.BlockSpec((g_rows.shape[0], features), lambda j, place: (0, j))]
-            + [vmem] * 2
+            + [once(scaled), once(out)]
             + [pl.BlockSpec((1, 1, features), lambda j, place: (j, 0, 0))],
             out_specs=pl.BlockSpec((features, width), lambda j, place: (j, 0)),
         ),
@@ -308,7 +301,7 @@
             transcendentals=0,
         ),
         name="weight_grads",
-    )(places, *heads, *tails, *g_tails, g_rows, scaled, out, gain)
+    )(places, *x_parts, g_rows, scaled, out, gain)
 
 
 def per_device(roll_rows, dest, lengths, clusters, log_prob_grad, gain, w_q, w_k, w_v, w_o_t):
@@ -418,11 +411,11 @@
     ]
     head_shards = shards(x_head, head_near, head_far2, after(head_end, raw1, *ga), z)
     raw0, inv0 = project(head_shards, w_k_parts, (), feature_count)
-    dqkv0, dqkv1, scales0, scales1, scaled, out = attention(
+    dqkv, scales, scaled, out = attention(
         (raw0, raw1), (inv0, inv1), ga, adv, cos, sin, start
     )
-    half = dqkv0.shape[0]
-    terms0 = input_terms(dqkv0, scales0, [x[:half] for x in head_shards])
+    half = row_count // (2 * BLOCK) * BLOCK
+    terms0 = input_terms(dqkv[:half], scales[:half], [x[:half] for x in head_shards])
     end0 = scatter_end(terms0)
     total0 = far_total(terms0, end0)
     step0 = scatter_far(total0)
@@ -442,8 +435,8 @@
     summed = lax.psum_scatter(after(weight_terms, end0), "fsdp", scatter_dimension=0, tiled=True)
 
     terms1 = input_terms(
-        after(dqkv1, end0),
-        scales1,
+        after(dqkv[half:], end0),
+        scales[half:],
         [jnp.concatenate([x[half:], y], axis=0) for x, y in zip(head_shards, tail_shards)],
     )
     end1 = scatter_end([*terms1[:3], after(terms1[3], end0)])

time: 376 us -> 364 us (0.968)
  Pallas kernels: 41.3 us -> 29.2 us
    pallas_call x1, Pallas kernels: 21.4 us -> 9.33 us  [attention(): pl.pallas_call(attention_kernel, out_shape=out_shape, in_specs=[vmem] * l...]
    unnamed x116 -> x114, local copies, waits for them, and re-layouts: 18.5 us -> 18.5 us
  transfers between devices with their start and end apart: 31 -> 31, of which waited for: 16 -> 16; matrix products, arithmetic and copies ran while one was open for 15% -> 16% of each run, Pallas kernels for 4% -> 4%
where the time goes in v1:
time: 364 us; the launch traced here: 361 us
  waiting for transfers between devices  154 us (42%)
  starting transfers between devices  77.2 us (21%)
  local copies, waits for them, and re-layouts  43.3 us (12%)
  Pallas kernels  29.2 us (8%)
  other arithmetic  22.6 us (6%)
  matrix products  19.4 us (5%)
  between operations  14.9 us (4%)
    ppermute x6, waiting for transfers between devices, gather_near(): return (lax.ppermute(own, 'tp', UP), lax.ppermute(own, 'tp', DOWN))  49 us
    ppermute x3, waiting for transfers between devices, gather_end(): return lax.ppermute(far2, 'tp', TO_ENDS)  33 us
    ppermute x6, starting transfers between devices, gather_near(): return (lax.ppermute(own, 'tp', UP), lax.ppermute(own, 'tp', DOWN))  24.5 us
    ppermute x3, waiting for transfers between devices, gather_far(): down2 = lax.ppermute(step1[1], 'tp', DOWN_MID)  20.5 us
    ppermute x2, waiting for transfers between devices, scatter_far(): lax.ppermute(total2, 'tp', UP_IN)  20.1 us
    unnamed x114, local copies, waits for them, and re-layouts  18.5 us
    ppermute x2, starting transfers between devices, scatter_near(): up3 = lax.ppermute(go_up.astype(jnp.bfloat16), 'tp', UP)  14.2 us
    pallas_call x1, Pallas kernels, weight_grads(): pl.pallas_call(weight_grad_kernel, out_shape=jax.ShapeDtypeStruct((4 * fe...  12.4 us
  transfers between devices with their start and end apart: 31, of which 16 were waited for; matrix products, arithmetic and copies ran while one was open for 16% of the time, Pallas kernels for 4%

profile of v1, /device:TPU:0, one launch (start us, length us, event | category | flops | bytes accessed | tf_op | source)
XLA Modules:
  0.0 361.1 jit_solution(5608193780193803466)
XLA Ops:
  12.9 5.2 %all-to-all-start = ((bf16[8,4,2]{1,2,0:T(2,128)(2,1)}), bf16[8,4,2]{1,2,0:T(2,128)(2,1)S(1)}, u32[]{:S(2)}, u32[]{:S(2)}) async-start(bf16[8,4,2]{1,2,0:T(2,128)(2,1)} %copy.41), calls=%async_computation | async-start | bytes 8192 | tf_op jit(solution)/shard_map/all_to_all | solution.py:343
  18.2 5.7 %gather_fusion = bf16[32,72,896]{2,1,0:T(8,128)(2,1)} fusion(bf16[32,72,896]{2,1,0:T(8,128)(2,1)} %param.10, s32[1024]{0:T(1024)S(1)} %pad_clamp_fusion.1), kind=kCustom, calls=%fused_computation | custom fusion | bytes 8257664 | tf_op jit(solution)/shard_map/jit(_take)/gather | solution.py:334
  36.8 15.9 %collective-permute-done.1 = bf16[256,896]{1,0:T(8,128)(2,1)} collective-permute-done((bf16[256,896]{1,0:T(8,128)(2,1)S(1)}, bf16[256,896]{1,0:T(8,128)(2,1)}, u32[]{:S(2)}, u32[]{:S(2)}) %collective-permute-start.1) | collective-permute-done | bytes 458784 | tf_op jit(solution)/shard_map/ppermute | solution.py:45
  54.1 13.7 %collective-permute-done.3 = bf16[256,896]{1,0:T(8,128)(2,1)} collective-permute-done((bf16[256,896]{1,0:T(8,128)(2,1)S(1)}, bf16[256,896]{1,0:T(8,128)(2,1)}, u32[]{:S(2)}, u32[]{:S(2)}) %collective-permute-start.3) | collective-permute-done | bytes 458784 | tf_op jit(solution)/shard_map/ppermute | solution.py:45
  71.0 6.0 %all-to-all-done.1 = bf16[32,72,896]{2,1,0:T(8,128)(2,1)} async-done(((bf16[32,72,896]{2,1,0:T(8,128)(2,1)}), bf16[32,72,896]{2,1,0:T(8,128)(2,1)}, u32[]{:S(2)}, u32[]{:S(2)}) %all-to-all-start.1) | async-done | bytes 4128800 | tf_op jit(solution)/shard_map/all_to_all | solution.py:335
  77.0 6.2 %gather_fusion.1 = bf16[768,896]{1,0:T(8,128)(2,1)S(1)} fusion(bf16[2304,896]{1,0:T(8,128)(2,1)} %bitcast.5, s32[1024]{0:T(1024)S(1)} %pad_clamp_fusion), kind=kCustom, calls=%fused_computation.1 | custom fusion | bytes 2755584 | tf_op jit(solution)/shard_map/jit(_take)/gather | solution.py:368
  87.6 12.1 %collective-permute-done.4 = bf16[256,896]{1,0:T(8,128)(2,1)} collective-permute-done((bf16[256,896]{1,0:T(8,128)(2,1)}, bf16[256,896]{1,0:T(8,128)(2,1)}, u32[]{:S(2)}, u32[]{:S(2)}) %collective-permute-start.4) | collective-permute-done | bytes 458784 | tf_op jit(solution)/shard_map/ppermute | solution.py:50
  103.9 12.1 %collective-permute-start.5 = (bf16[512,896]{1,0:T(8,128)(2,1)S(1)}, bf16[512,896]{1,0:T(8,128)(2,1)}, u32[]{:S(2)}, u32[]{:S(2)}) collective-permute-start(bf16[512,896]{1,0:T(8,128)(2,1)S(1)} %slice.118.refs_0_), channel_id=1, source_target_pairs={{0,1},{1,2},{2,3},{4,5},{5,6},{6,7},{8,9},{9,10},{10,11},{12,13},{... | collective-permute-start | bytes 2752520 | tf_op jit(solution)/shard_map/ppermute | solution.py:45
  122.4 16.3 %collective-permute-done.6 = bf16[512,896]{1,0:T(8,128)(2,1)} collective-permute-done((bf16[512,896]{1,0:T(8,128)(2,1)S(1)}, bf16[512,896]{1,0:T(8,128)(2,1)}, u32[]{:S(2)}, u32[]{:S(2)}) %collective-permute-start.6) | collective-permute-done | bytes 917536 | tf_op jit(solution)/shard_map/ppermute | solution.py:45
  140.0 8.4 %collective-permute-done.9 = bf16[256,896]{1,0:T(8,128)(2,1)S(1)} collective-permute-done((bf16[256,896]{1,0:T(8,128)(2,1)}, bf16[256,896]{1,0:T(8,128)(2,1)S(1)}, u32[]{:S(2)}, u32[]{:S(2)}) %collective-permute-start.9) | collective-permute-done | bytes 458784 | tf_op jit(solution)/shard_map/ppermute | solution.py:50
  152.0 6.3 %collective-permute-done.12 = bf16[256,896]{1,0:T(8,128)(2,1)S(1)} collective-permute-done((bf16[256,896]{1,0:T(8,128)(2,1)S(1)}, bf16[256,896]{1,0:T(8,128)(2,1)S(1)}, u32[]{:S(2)}, u32[]{:S(2)}) %collective-permute-start.12) | collective-permute-done | bytes 458784 | tf_op jit(solution)/shard_map/ppermute | solution.py:55
  163.7 21.6 %collective-permute-done.13 = bf16[256,896]{1,0:T(8,128)(2,1)} collective-permute-done((bf16[256,896]{1,0:T(8,128)(2,1)S(1)}, bf16[256,896]{1,0:T(8,128)(2,1)}, u32[]{:S(2)}, u32[]{:S(2)}) %collective-permute-start.13) | collective-permute-done | bytes 458784 | tf_op jit(solution)/shard_map/ppermute | solution.py:55
  206.8 5.1 %collective-permute-done.14 = bf16[512,896]{1,0:T(8,128)(2,1)} collective-permute-done((bf16[512,896]{1,0:T(8,128)(2,1)}, bf16[512,896]{1,0:T(8,128)(2,1)}, u32[]{:S(2)}, u32[]{:S(2)}) %collective-permute-start.14) | collective-permute-done | bytes 917536 | tf_op jit(solution)/shard_map/ppermute | solution.py:55
  214.1 5.6 %project.3 = (f32[512,768]{1,0:T(8,128)S(1)}, f32[512,1]{1,0:T(8,128)S(1)}) custom-call(bf16[512,896]{1,0:T(8,128)(2,1)S(1)} %copy-done.30, bf16[512,896]{1,0:T(8,128)(2,1)S(1)} %get-tuple-element.60.refs_1_, bf16[512,896]{1,0:T(8,128)(2,1)} %broadcast_select_fusion.refs_2_, bf16[512,896]{1,0:T(8,128)(2,1)S(1)} %get-tuple-element.59.refs_3_, ...), custom_call_target="tpu_custom_call" | custom-call | flops 2818572288 | bytes 12320768 | tf_op jit(solution)/shard_map/project/pallas_call | solution.py:240
  219.8 9.3 %attention.1 = (bf16[768,768]{1,0:T(8,128)(2,1)S(1)}, f32[768,2]{1,0:T(8,128)S(1)}, bf16[768,768]{1,0:T(8,128)(2,1)S(1)}, bf16[768,512]{1,0:T(8,128)(2,1)S(1)}) custom-call(f32[512,768]{1,0:T(8,128)S(1)} %get-tuple-element.36.refs_0_, f32[256,768]{1,0:T(8,128)S(1)} %get-tuple-element.33.refs_1_, f32[512,1]{1,0:T(8,128)S(1)} %get-tuple-element.37.refs_2_, ...), custom_call_target="tpu_custom_call" | custom-call | flops 1207959552 | bytes 7077888 | tf_op jit(solution)/shard_map/attention/pallas_call | solution.py:198
  248.8 12.4 %weight_grads.1 = bf16[3584,1280]{1,0:T(8,128)(2,1)} custom-call(s32[4]{0:T(128)S(1)} %pad_add_fusion.place_ref, bf16[512,896]{1,0:T(8,128)(2,1)S(1)} %copy-done.31, bf16[512,896]{1,0:T(8,128)(2,1)S(1)} %copy-done.24, bf16[512,896]{1,0:T(8,128)(2,1)} %broadcast_select_fusion.refs_2_, bf16[512,896]{1,0:T(8,128)(2,1)S(1)} %copy-done.27, ...), custom_call_target="tpu_custom_call" | custom-call | flops 7046430720 | bytes 20185088 | tf_op jit(solution)/shard_map/weight_grads/pallas_call | solution.py:285
  272.8 9.8 %collective-permute-done.20 = bf16[384,896]{1,0:T(8,128)(2,1)S(1)} collective-permute-done((bf16[384,896]{1,0:T(8,128)(2,1)S(1)}, bf16[384,896]{1,0:T(8,128)(2,1)S(1)}, u32[]{:S(2)}, u32[]{:S(2)}) %collective-permute-start.20) | collective-permute-done | bytes 688160 | tf_op jit(solution)/shard_map/ppermute | solution.py:70
  282.6 10.5 %collective-permute-done.16 = bf16[384,896]{1,0:T(8,128)(2,1)S(1)} collective-permute-done((bf16[384,896]{1,0:T(8,128)(2,1)S(1)}, bf16[384,896]{1,0:T(8,128)(2,1)S(1)}, u32[]{:S(2)}, u32[]{:S(2)}) %collective-permute-start.16) | collective-permute-done | bytes 688160 | tf_op jit(solution)/shard_map/ppermute | solution.py:78
  296.6 5.2 %collective-permute-start.17 = (bf16[384,896]{1,0:T(8,128)(2,1)S(1)}, bf16[384,896]{1,0:T(8,128)(2,1)S(1)}, u32[]{:S(2)}, u32[]{:S(2)}) collective-permute-start(bf16[384,896]{1,0:T(8,128)(2,1)S(1)} %get-tuple-element.63), channel_id=1, source_target_pairs={{0,1},{1,2},{2,3},{4,5},{5,6},{6,7},{8,9},{9,10},{10,11},{12,13},{... | collective-permute-start | bytes 2064392 | tf_op jit(solution)/shard_map/ppermute | solution.py:87
  302.2 7.6 %collective-permute-start.21 = (bf16[384,896]{1,0:T(8,128)(2,1)S(1)}, bf16[384,896]{1,0:T(8,128)(2,1)S(1)}, u32[]{:S(2)}, u32[]{:S(2)}) collective-permute-start(bf16[384,896]{1,0:T(8,128)(2,1)S(1)} %add_convert_fusion.2), channel_id=1, source_target_pairs={{0,1},{1,2},{4,5},{5,6},{8,9},{9,10},{12,13},{13,14},{16,17},{17,1... | collective-permute-start | bytes 2064392 | tf_op jit(solution)/shard_map/ppermute | solution.py:78
  312.5 5.2 %collective-permute-done.17 = bf16[384,896]{1,0:T(8,128)(2,1)S(1)} collective-permute-done((bf16[384,896]{1,0:T(8,128)(2,1)S(1)}, bf16[384,896]{1,0:T(8,128)(2,1)S(1)}, u32[]{:S(2)}, u32[]{:S(2)}) %collective-permute-start.17) | collective-permute-done | bytes 688160 | tf_op jit(solution)/shard_map/ppermute | solution.py:87
  317.9 9.6 %collective-permute-done.21 = bf16[384,896]{1,0:T(8,128)(2,1)S(1)} collective-permute-done((bf16[384,896]{1,0:T(8,128)(2,1)S(1)}, bf16[384,896]{1,0:T(8,128)(2,1)S(1)}, u32[]{:S(2)}, u32[]{:S(2)}) %collective-permute-start.21) | collective-permute-done | bytes 688160 | tf_op jit(solution)/shard_map/ppermute | solution.py:78
  329.2 9.0 %collective-permute-start.22 = (bf16[384,896]{1,0:T(8,128)(2,1)S(1)}, bf16[384,896]{1,0:T(8,128)(2,1)S(1)}, u32[]{:S(2)}, u32[]{:S(2)}) collective-permute-start(bf16[384,896]{1,0:T(8,128)(2,1)S(1)} %get-tuple-element.61), channel_id=1, source_target_pairs={{0,1},{1,2},{2,3},{4,5},{5,6},{6,7},{8,9},{9,10},{10,11},{12,13},{... | collective-permute-start | bytes 2064392 | tf_op jit(solution)/shard_map/ppermute | solution.py:87
  339.0 8.8 %collective-permute-done.24 = bf16[384,896]{1,0:T(8,128)(2,1)S(1)} collective-permute-done((bf16[384,896]{1,0:T(8,128)(2,1)S(1)}, bf16[384,896]{1,0:T(8,128)(2,1)S(1)}, u32[]{:S(2)}, u32[]{:S(2)}) %collective-permute-start.24) | collective-permute-done | bytes 688160 | tf_op jit(solution)/shard_map/ppermute | solution.py:88
  (241 shorter events, 118.5 us)
Async XLA Ops:
  7.2 113.2 %all-gather.4.cloned.1.call-start = ((), (), s32[]{:S(2)}) async-start(), calls=%async_computation.3 | async-start | bytes 4587520 | tf_op jit(solution)/shard_map/all_gather | solution.py:321
  9.6 181.8 %all-gather.8.cloned.1.call-start = ((), (), s32[]{:S(2)}) async-start(), calls=%async_computation.5 | async-start | bytes 4128768 | tf_op jit(solution)/shard_map/all_gather | solution.py:383
  10.3 189.8 %all-gather.6.cloned.1.call-start = ((), (), s32[]{:S(2)}) async-start(), calls=%async_computation.4 | async-start | bytes 6193152 | tf_op jit(solution)/shard_map/all_gather | solution.py:380
  23.9 53.1 %all-to-all-start.1 = ((bf16[32,72,896]{2,1,0:T(8,128)(2,1)}), bf16[32,72,896]{2,1,0:T(8,128)(2,1)}, u32[]{:S(2)}, u32[]{:S(2)}) async-start(bf16[32,72,896]{2,1,0:T(8,128)(2,1)} %gather_fusion), calls=%async_computation.1 | async-start | bytes 8257536 | tf_op jit(solution)/shard_map/all_to_all | solution.py:335
  28.6 322.1 %reduce-scatter.2.cloned.1.call-start = ((), (), s32[]{:S(2)}) async-start(), calls=%async_computation.6 | async-start | bytes 10321920 | tf_op jit(solution)/shard_map/reduce_scatter | solution.py:435
  28.7 24.0 %collective-permute-start.1 = (bf16[256,896]{1,0:T(8,128)(2,1)S(1)}, bf16[256,896]{1,0:T(8,128)(2,1)}, u32[]{:S(2)}, u32[]{:S(2)}) collective-permute-start(bf16[256,896]{1,0:T(8,128)(2,1)S(1)} %slice.95.refs_8_), channel_id=1, source_target_pairs={{0,1},{1,2},{2,3},{4,5},{5,6},{6,7},{8,9},{9,10},{10,11},{12,13},{... | collective-permute-start | bytes 1376264 | tf_op jit(solution)/shard_map/ppermute | solution.py:45
  33.0 34.8 %collective-permute-start.3 = (bf16[256,896]{1,0:T(8,128)(2,1)S(1)}, bf16[256,896]{1,0:T(8,128)(2,1)}, u32[]{:S(2)}, u32[]{:S(2)}) collective-permute-start(bf16[256,896]{1,0:T(8,128)(2,1)S(1)} %slice.95.refs_8_), channel_id=1, source_target_pairs={{1,0},{2,1},{3,2},{5,4},{6,5},{7,6},{9,8},{10,9},{11,10},{13,12},{... | collective-permute-start | bytes 1376264 | tf_op jit(solution)/shard_map/ppermute | solution.py:45
  52.7 34.9 %collective-permute-start.2 = (bf16[256,896]{1,0:T(8,128)(2,1)}, bf16[256,896]{1,0:T(8,128)(2,1)}, u32[]{:S(2)}, u32[]{:S(2)}) collective-permute-start(bf16[256,896]{1,0:T(8,128)(2,1)} %collective-permute-done.1), channel_id=1, source_target_pairs={{1,2},{2,3},{5,6},{6,7},{9,10},{10,11},{13,14},{14,15},{17,18},{18... | collective-permute-start | bytes 1376264 | tf_op jit(solution)/shard_map/ppermute | solution.py:49
  67.8 31.9 %collective-permute-start.4 = (bf16[256,896]{1,0:T(8,128)(2,1)}, bf16[256,896]{1,0:T(8,128)(2,1)}, u32[]{:S(2)}, u32[]{:S(2)}) collective-permute-start(bf16[256,896]{1,0:T(8,128)(2,1)} %collective-permute-done.3), channel_id=1, source_target_pairs={{1,0},{2,1},{5,4},{6,5},{9,8},{10,9},{13,12},{14,13},{17,16},{18,1... | collective-permute-start | bytes 1376264 | tf_op jit(solution)/shard_map/ppermute | solution.py:50
  102.6 36.1 %collective-permute-start.6 = (bf16[512,896]{1,0:T(8,128)(2,1)S(1)}, bf16[512,896]{1,0:T(8,128)(2,1)}, u32[]{:S(2)}, u32[]{:S(2)}) collective-permute-start(bf16[512,896]{1,0:T(8,128)(2,1)S(1)} %slice.118.refs_0_), channel_id=1, source_target_pairs={{1,0},{2,1},{3,2},{5,4},{6,5},{7,6},{9,8},{10,9},{11,10},{13,12},{... | collective-permute-start | bytes 2752520 | tf_op jit(solution)/shard_map/ppermute | solution.py:45
  103.9 46.5 %collective-permute-start.5 = (bf16[512,896]{1,0:T(8,128)(2,1)S(1)}, bf16[512,896]{1,0:T(8,128)(2,1)}, u32[]{:S(2)}, u32[]{:S(2)}) collective-permute-start(bf16[512,896]{1,0:T(8,128)(2,1)S(1)} %slice.118.refs_0_), channel_id=1, source_target_pairs={{0,1},{1,2},{2,3},{4,5},{5,6},{6,7},{8,9},{9,10},{10,11},{12,13},{... | collective-permute-start | bytes 2752520 | tf_op jit(solution)/shard_map/ppermute | solution.py:45
  119.0 29.4 %collective-permute-start.9 = (bf16[256,896]{1,0:T(8,128)(2,1)}, bf16[256,896]{1,0:T(8,128)(2,1)S(1)}, u32[]{:S(2)}, u32[]{:S(2)}) collective-permute-start(bf16[256,896]{1,0:T(8,128)(2,1)} %collective-permute-done.8), channel_id=1, source_target_pairs={{1,0},{2,1},{5,4},{6,5},{9,8},{10,9},{13,12},{14,13},{17,16},{18,1... | collective-permute-start | bytes 1376264 | tf_op jit(solution)/shard_map/ppermute | solution.py:50
  120.4 28.8 %collective-permute-start.7 = (bf16[256,896]{1,0:T(8,128)(2,1)}, bf16[256,896]{1,0:T(8,128)(2,1)S(1)}, u32[]{:S(2)}, u32[]{:S(2)}) collective-permute-start(bf16[256,896]{1,0:T(8,128)(2,1)} %collective-permute-done), channel_id=1, source_target_pairs={{1,2},{2,3},{5,6},{6,7},{9,10},{10,11},{13,14},{14,15},{17,18},{18... | collective-permute-start | bytes 1376264 | tf_op jit(solution)/shard_map/ppermute | solution.py:49
  121.1 37.2 %collective-permute-start.12 = (bf16[256,896]{1,0:T(8,128)(2,1)S(1)}, bf16[256,896]{1,0:T(8,128)(2,1)S(1)}, u32[]{:S(2)}, u32[]{:S(2)}) collective-permute-start(bf16[256,896]{1,0:T(8,128)(2,1)S(1)} %broadcast_select_fusion.5.refs_10_), channel_id=1, source_target_pairs={{2,3},{1,0},{6,7},{5,4},{10,11},{9,8},{14,15},{13,12},{18,19},{17,... | collective-permute-start | bytes 1376264 | tf_op jit(solution)/shard_map/ppermute | solution.py:55
  138.7 48.9 %collective-permute-start.11 = (bf16[512,896]{1,0:T(8,128)(2,1)}, bf16[512,896]{1,0:T(8,128)(2,1)}, u32[]{:S(2)}, u32[]{:S(2)}) collective-permute-start(bf16[512,896]{1,0:T(8,128)(2,1)} %collective-permute-done.6), channel_id=1, source_target_pairs={{1,0},{2,1},{5,4},{6,5},{9,8},{10,9},{13,12},{14,13},{17,16},{18,1... | collective-permute-start | bytes 2752520 | tf_op jit(solution)/shard_map/ppermute | solution.py:50
  150.3 37.3 %collective-permute-start.10 = (bf16[512,896]{1,0:T(8,128)(2,1)}, bf16[512,896]{1,0:T(8,128)(2,1)}, u32[]{:S(2)}, u32[]{:S(2)}) collective-permute-start(bf16[512,896]{1,0:T(8,128)(2,1)} %collective-permute-done.5), channel_id=1, source_target_pairs={{1,2},{2,3},{5,6},{6,7},{9,10},{10,11},{13,14},{14,15},{17,18},{18... | collective-permute-start | bytes 2752520 | tf_op jit(solution)/shard_map/ppermute | solution.py:49
  159.0 26.3 %collective-permute-start.13 = (bf16[256,896]{1,0:T(8,128)(2,1)S(1)}, bf16[256,896]{1,0:T(8,128)(2,1)}, u32[]{:S(2)}, u32[]{:S(2)}) collective-permute-start(bf16[256,896]{1,0:T(8,128)(2,1)S(1)} %broadcast_select_fusion.4.refs_2_.refs_6_), channel_id=1, source_target_pairs={{2,3},{1,0},{6,7},{5,4},{10,11},{9,8},{14,15},{13,12},{18,19},{17,... | collective-permute-start | bytes 1376264 | tf_op jit(solution)/shard_map/ppermute | solution.py:55
  189.9 22.1 %collective-permute-start.14 = (bf16[512,896]{1,0:T(8,128)(2,1)}, bf16[512,896]{1,0:T(8,128)(2,1)}, u32[]{:S(2)}, u32[]{:S(2)}) collective-permute-start(bf16[512,896]{1,0:T(8,128)(2,1)} %broadcast_select_fusion.refs_2_), channel_id=1, source_target_pairs={{2,3},{1,0},{6,7},{5,4},{10,11},{9,8},{14,15},{13,12},{18,19},{17,... | collective-permute-start | bytes 2752520 | tf_op jit(solution)/shard_map/ppermute | solution.py:55
  231.3 29.9 %collective-permute-start.15 = (bf16[384,896]{1,0:T(8,128)(2,1)}, bf16[384,896]{1,0:T(8,128)(2,1)}, u32[]{:S(2)}, u32[]{:S(2)}) collective-permute-start(bf16[384,896]{1,0:T(8,128)(2,1)} %subtract_convert_fusion.3), channel_id=1, source_target_pairs={{3,2},{0,1},{7,6},{4,5},{11,10},{8,9},{15,14},{12,13},{19,18},{16,... | collective-permute-start | bytes 2064392 | tf_op jit(solution)/shard_map/ppermute | solution.py:70
  268.9 24.2 %collective-permute-start.16 = (bf16[384,896]{1,0:T(8,128)(2,1)S(1)}, bf16[384,896]{1,0:T(8,128)(2,1)S(1)}, u32[]{:S(2)}, u32[]{:S(2)}) collective-permute-start(bf16[384,896]{1,0:T(8,128)(2,1)S(1)} %add_convert_fusion.5), channel_id=1, source_target_pairs={{0,1},{1,2},{4,5},{5,6},{8,9},{9,10},{12,13},{13,14},{16,17},{17,1... | collective-permute-start | bytes 2064392 | tf_op jit(solution)/shard_map/ppermute | solution.py:78
  270.3 22.8 %collective-permute-start.18 = (bf16[384,896]{1,0:T(8,128)(2,1)S(1)}, bf16[384,896]{1,0:T(8,128)(2,1)S(1)}, u32[]{:S(2)}, u32[]{:S(2)}) collective-permute-start(bf16[384,896]{1,0:T(8,128)(2,1)S(1)} %add_convert_fusion.5), channel_id=1, source_target_pairs={{3,2},{2,1},{7,6},{6,5},{11,10},{10,9},{15,14},{14,13},{19,18},{18... | collective-permute-start | bytes 2064392 | tf_op jit(solution)/shard_map/ppermute | solution.py:78
  296.6 21.0 %collective-permute-start.17 = (bf16[384,896]{1,0:T(8,128)(2,1)S(1)}, bf16[384,896]{1,0:T(8,128)(2,1)S(1)}, u32[]{:S(2)}, u32[]{:S(2)}) collective-permute-start(bf16[384,896]{1,0:T(8,128)(2,1)S(1)} %get-tuple-element.63), channel_id=1, source_target_pairs={{0,1},{1,2},{2,3},{4,5},{5,6},{6,7},{8,9},{9,10},{10,11},{12,13},{... | collective-permute-start | bytes 2064392 | tf_op jit(solution)/shard_map/ppermute | solution.py:87
  302.2 25.3 %collective-permute-start.21 = (bf16[384,896]{1,0:T(8,128)(2,1)S(1)}, bf16[384,896]{1,0:T(8,128)(2,1)S(1)}, u32[]{:S(2)}, u32[]{:S(2)}) collective-permute-start(bf16[384,896]{1,0:T(8,128)(2,1)S(1)} %add_convert_fusion.2), channel_id=1, source_target_pairs={{0,1},{1,2},{4,5},{5,6},{8,9},{9,10},{12,13},{13,14},{16,17},{17,1... | collective-permute-start | bytes 2064392 | tf_op jit(solution)/shard_map/ppermute | solution.py:78
  327.9 20.0 %collective-permute-start.24 = (bf16[384,896]{1,0:T(8,128)(2,1)S(1)}, bf16[384,896]{1,0:T(8,128)(2,1)S(1)}, u32[]{:S(2)}, u32[]{:S(2)}) collective-permute-start(bf16[384,896]{1,0:T(8,128)(2,1)S(1)} %get-tuple-element.62), channel_id=1, source_target_pairs={{1,0},{2,1},{3,2},{5,4},{6,5},{7,6},{9,8},{10,9},{11,10},{13,12},{... | collective-permute-start | bytes 2064392 | tf_op jit(solution)/shard_map/ppermute | solution.py:88
  (64 other events, 695.5 us)
Sparse Core Ops, SparseCore 0:
  9.7 94.1 all-gather.3
  105.7 34.4 all-gather.7
  142.2 42.2 all-gather.5
  261.4 78.3 reduce-scatter.1

commit v2 on v1

--- a/solution.py
+++ b/solution.py
@@ -294,7 +294,7 @@
             + [pl.BlockSpec((1, 1, features), lambda j, place: (j, 0, 0))],
             out_specs=pl.BlockSpec((features, width), lambda j, place: (j, 0)),
         ),
-        compiler_params=pltpu.CompilerParams(vmem_limit_bytes=40 * 1024 * 1024),
+        compiler_params=pltpu.CompilerParams(vmem_limit_bytes=58 * 1024 * 1024),
         cost_estimate=pl.CostEstimate(
             flops=2 * scaled.shape[0] * 4 * features * width,
             bytes_accessed=4 * features * (4 * scaled.shape[0] + 2 * width),
@@ -409,8 +409,11 @@
             for k in range(4)
         ),
     ]
-    head_shards = shards(x_head, head_near, head_far2, after(head_end, raw1, *ga), z)
-    raw0, inv0 = project(head_shards, w_k_parts, (), feature_count)
+    near = jnp.where(z % 2 == 1, *head_near)
+    early = project([x_head, near, head_far2], w_k_parts[:3], (), 0)
+    head_shards = shards(x_head, head_near, head_far2, after(head_end, raw1, *early, *ga), z)
+    head_shards[1] = near
+    raw0, inv0 = project(head_shards[3:], w_k_parts[3:], early, feature_count)
     dqkv, scales, scaled, out = attention(
         (raw0, raw1), (inv0, inv1), ga, adv, cos, sin, start
     )
@@ -435,7 +438,7 @@
     summed = lax.psum_scatter(after(weight_terms, end0), "fsdp", scatter_dimension=0, tiled=True)
 
     terms1 = input_terms(
-        after(dqkv[half:], end0),
+        after(dqkv[half:], total0),
         scales[half:],
         [jnp.concatenate([x[half:], y], axis=0) for x, y in zip(head_shards, tail_shards)],
     )

time: 364 us -> 353 us (0.970)
  local copies, waits for them, and re-layouts: 43.3 us -> 29.3 us
    unnamed x114 -> x96, local copies, waits for them, and re-layouts: 18.5 us -> 3.2 us
    ppermute x3, waiting for transfers between devices: 33 us -> 25.6 us  [gather_end(): return lax.ppermute(far2, 'tp', TO_ENDS)]
    ppermute x2, starting transfers between devices: 3.66 us -> 7.42 us  [scatter_end(): return lax.ppermute(parts[3], 'tp', FROM_ENDS)]
    pallas_call x2 -> x3, Pallas kernels: 7.49 us -> 6.73 us  [project(): pl.pallas_call(functools.partial(project_kernel, len(parts), feature_coun...]
  transfers between devices with their start and end apart: 31 -> 31, of which waited for: 16 -> 16; matrix products, arithmetic and copies ran while one was open for 16% -> 18% of each run, Pallas kernels for 4% -> 6%
where the time goes in v2:
time: 353 us; the launch traced here: 350 us
  waiting for transfers between devices  152 us (43%)
  starting transfers between devices  77.6 us (22%)
  Pallas kernels  31.2 us (9%)
  local copies, waits for them, and re-layouts  29.3 us (8%)
  other arithmetic  26.1 us (7%)
  matrix products  19.6 us (6%)
  between operations  14.8 us (4%)
    ppermute x6, waiting for transfers between devices, gather_near(): return (lax.ppermute(own, 'tp', UP), lax.ppermute(own, 'tp', DOWN))  49.3 us
    ppermute x3, waiting for transfers between devices, gather_end(): return lax.ppermute(far2, 'tp', TO_ENDS)  25.6 us
    ppermute x6, starting transfers between devices, gather_near(): return (lax.ppermute(own, 'tp', UP), lax.ppermute(own, 'tp', DOWN))  22.6 us
    ppermute x2, waiting for transfers between devices, scatter_far(): lax.ppermute(total2, 'tp', UP_IN)  20.9 us
    ppermute x3, waiting for transfers between devices, gather_far(): down2 = lax.ppermute(step1[1], 'tp', DOWN_MID)  19.6 us
    pallas_call x1, Pallas kernels, weight_grads(): pl.pallas_call(weight_grad_kernel, out_shape=jax.ShapeDtypeStruct((4 * fe...  15.2 us
    ppermute x2, starting transfers between devices, scatter_near(): up3 = lax.ppermute(go_up.astype(jnp.bfloat16), 'tp', UP)  13.7 us
    ppermute x2, waiting for transfers between devices, scatter_end(): return lax.ppermute(parts[3], 'tp', FROM_ENDS)  12 us
  transfers between devices with their start and end apart: 31, of which 16 were waited for; matrix products, arithmetic and copies ran while one was open for 18% of the time, Pallas kernels for 6%

profile of v2, /device:TPU:0, one launch (start us, length us, event | category | flops | bytes accessed | tf_op | source)
XLA Modules:
  0.0 350.4 jit_solution(1812405639562080387)
XLA Ops:
  12.9 5.2 %all-to-all-start = ((bf16[8,4,2]{1,2,0:T(2,128)(2,1)}), bf16[8,4,2]{1,2,0:T(2,128)(2,1)S(1)}, u32[]{:S(2)}, u32[]{:S(2)}) async-start(bf16[8,4,2]{1,2,0:T(2,128)(2,1)} %copy.41), calls=%async_computation | async-start | bytes 8192 | tf_op jit(solution)/shard_map/all_to_all | solution.py:343
  18.2 5.7 %gather_fusion = bf16[32,72,896]{2,1,0:T(8,128)(2,1)} fusion(bf16[32,72,896]{2,1,0:T(8,128)(2,1)} %param.10, s32[1024]{0:T(1024)S(1)} %pad_clamp_fusion.1), kind=kCustom, calls=%fused_computation | custom fusion | bytes 8257664 | tf_op jit(solution)/shard_map/jit(_take)/gather | solution.py:334
  23.9 4.7 %all-to-all-start.1 = ((bf16[32,72,896]{2,1,0:T(8,128)(2,1)}), bf16[32,72,896]{2,1,0:T(8,128)(2,1)}, u32[]{:S(2)}, u32[]{:S(2)}) async-start(bf16[32,72,896]{2,1,0:T(8,128)(2,1)} %gather_fusion), calls=%async_computation.1 | async-start | bytes 8257536 | tf_op jit(solution)/shard_map/all_to_all | solution.py:335
  36.1 16.7 %collective-permute-done.1 = bf16[256,896]{1,0:T(8,128)(2,1)S(1)} collective-permute-done((bf16[256,896]{1,0:T(8,128)(2,1)S(1)}, bf16[256,896]{1,0:T(8,128)(2,1)S(1)}, u32[]{:S(2)}, u32[]{:S(2)}) %collective-permute-start.1) | collective-permute-done | bytes 458784 | tf_op jit(solution)/shard_map/ppermute | solution.py:45
  54.1 12.8 %collective-permute-done.3 = bf16[256,896]{1,0:T(8,128)(2,1)S(1)} collective-permute-done((bf16[256,896]{1,0:T(8,128)(2,1)S(1)}, bf16[256,896]{1,0:T(8,128)(2,1)S(1)}, u32[]{:S(2)}, u32[]{:S(2)}) %collective-permute-start.3) | collective-permute-done | bytes 458784 | tf_op jit(solution)/shard_map/ppermute | solution.py:45
  70.2 6.9 %all-to-all-done.1 = bf16[32,72,896]{2,1,0:T(8,128)(2,1)} async-done(((bf16[32,72,896]{2,1,0:T(8,128)(2,1)}), bf16[32,72,896]{2,1,0:T(8,128)(2,1)}, u32[]{:S(2)}, u32[]{:S(2)}) %all-to-all-start.1) | async-done | bytes 4128800 | tf_op jit(solution)/shard_map/all_to_all | solution.py:335
  77.1 6.9 %gather_fusion.1 = bf16[768,896]{1,0:T(8,128)(2,1)} fusion(bf16[2304,896]{1,0:T(8,128)(2,1)} %bitcast.5, s32[1024]{0:T(1024)S(1)} %pad_clamp_fusion), kind=kCustom, calls=%fused_computation.1 | custom fusion | bytes 2755584 | tf_op jit(solution)/shard_map/jit(_take)/gather | solution.py:368
  88.5 11.0 %collective-permute-done.4 = bf16[256,896]{1,0:T(8,128)(2,1)} collective-permute-done((bf16[256,896]{1,0:T(8,128)(2,1)S(1)}, bf16[256,896]{1,0:T(8,128)(2,1)}, u32[]{:S(2)}, u32[]{:S(2)}) %collective-permute-start.4) | collective-permute-done | bytes 458784 | tf_op jit(solution)/shard_map/ppermute | solution.py:50
  104.2 11.6 %collective-permute-start.6 = (bf16[512,896]{1,0:T(8,128)(2,1)S(1)}, bf16[512,896]{1,0:T(8,128)(2,1)}, u32[]{:S(2)}, u32[]{:S(2)}) collective-permute-start(bf16[512,896]{1,0:T(8,128)(2,1)S(1)} %slice.118.refs_0_), channel_id=1, source_target_pairs={{0,1},{1,2},{2,3},{4,5},{5,6},{6,7},{8,9},{9,10},{10,11},{12,13},{... | collective-permute-start | bytes 2752520 | tf_op jit(solution)/shard_map/ppermute | solution.py:45
  122.7 16.3 %collective-permute-done.5 = bf16[512,896]{1,0:T(8,128)(2,1)} collective-permute-done((bf16[512,896]{1,0:T(8,128)(2,1)S(1)}, bf16[512,896]{1,0:T(8,128)(2,1)}, u32[]{:S(2)}, u32[]{:S(2)}) %collective-permute-start.5) | collective-permute-done | bytes 917536 | tf_op jit(solution)/shard_map/ppermute | solution.py:45
  140.3 8.5 %collective-permute-done.9 = bf16[256,896]{1,0:T(8,128)(2,1)} collective-permute-done((bf16[256,896]{1,0:T(8,128)(2,1)}, bf16[256,896]{1,0:T(8,128)(2,1)}, u32[]{:S(2)}, u32[]{:S(2)}) %collective-permute-start.9) | collective-permute-done | bytes 458784 | tf_op jit(solution)/shard_map/ppermute | solution.py:50
  153.5 5.1 %collective-permute-done.12 = bf16[256,896]{1,0:T(8,128)(2,1)S(1)} collective-permute-done((bf16[256,896]{1,0:T(8,128)(2,1)}, bf16[256,896]{1,0:T(8,128)(2,1)S(1)}, u32[]{:S(2)}, u32[]{:S(2)}) %collective-permute-start.12) | collective-permute-done | bytes 458784 | tf_op jit(solution)/shard_map/ppermute | solution.py:55
  165.3 20.1 %collective-permute-done.13 = bf16[256,896]{1,0:T(8,128)(2,1)S(1)} collective-permute-done((bf16[256,896]{1,0:T(8,128)(2,1)S(1)}, bf16[256,896]{1,0:T(8,128)(2,1)S(1)}, u32[]{:S(2)}, u32[]{:S(2)}) %collective-permute-start.13) | collective-permute-done | bytes 458784 | tf_op jit(solution)/shard_map/ppermute | solution.py:55
  215.3 9.3 %attention.1 = (bf16[768,768]{1,0:T(8,128)(2,1)S(1)}, f32[768,2]{1,0:T(8,128)S(1)}, bf16[768,768]{1,0:T(8,128)(2,1)S(1)}, bf16[768,512]{1,0:T(8,128)(2,1)S(1)}) custom-call(f32[512,768]{1,0:T(8,128)S(1)} %get-tuple-element.40.refs_0_, f32[256,768]{1,0:T(8,128)S(1)} %get-tuple-element.35.refs_1_, f32[512,1]{1,0:T(8,128)S(1)} %get-tuple-element.41.refs_2_, ...), custom_call_target="tpu_custom_call" | custom-call | flops 1207959552 | bytes 7077888 | tf_op jit(solution)/shard_map/attention/pallas_call | solution.py:198
  226.7 6.1 %collective-permute-start.15 = (bf16[384,896]{1,0:T(8,128)(2,1)}, bf16[384,896]{1,0:T(8,128)(2,1)}, u32[]{:S(2)}, u32[]{:S(2)}) collective-permute-start(bf16[384,896]{1,0:T(8,128)(2,1)} %subtract_convert_fusion.5), channel_id=1, source_target_pairs={{3,2},{0,1},{7,6},{4,5},{11,10},{8,9},{15,14},{12,13},{19,18},{16,... | collective-permute-start | bytes 2064392 | tf_op jit(solution)/shard_map/ppermute | solution.py:70
  234.1 15.2 %weight_grads.1 = bf16[3584,1280]{1,0:T(8,128)(2,1)} custom-call(s32[4]{0:T(128)} %pad_add_fusion.place_ref, bf16[512,896]{1,0:T(8,128)(2,1)} %copy-done.21, bf16[512,896]{1,0:T(8,128)(2,1)} %broadcast_select_fusion.refs_1_, bf16[512,896]{1,0:T(8,128)(2,1)} %broadcast_select_fusion.1.refs_2_, bf16[512,896]{1,0:T(8,128)(2,1)} %copy-done.4, ...), custom_call_target="tpu_custom_call" | custom-call | flops 7046430720 | bytes 20185088 | tf_op jit(solution)/shard_map/weight_grads/pallas_call | solution.py:285
  259.1 12.0 %collective-permute-done.20 = bf16[384,896]{1,0:T(8,128)(2,1)S(1)} collective-permute-done((bf16[384,896]{1,0:T(8,128)(2,1)S(1)}, bf16[384,896]{1,0:T(8,128)(2,1)S(1)}, u32[]{:S(2)}, u32[]{:S(2)}) %collective-permute-start.20) | collective-permute-done | bytes 688160 | tf_op jit(solution)/shard_map/ppermute | solution.py:70
  271.0 11.0 %collective-permute-done.16 = bf16[384,896]{1,0:T(8,128)(2,1)S(1)} collective-permute-done((bf16[384,896]{1,0:T(8,128)(2,1)S(1)}, bf16[384,896]{1,0:T(8,128)(2,1)S(1)}, u32[]{:S(2)}, u32[]{:S(2)}) %collective-permute-start.16) | collective-permute-done | bytes 688160 | tf_op jit(solution)/shard_map/ppermute | solution.py:78
  285.6 5.3 %collective-permute-start.17 = (bf16[384,896]{1,0:T(8,128)(2,1)S(1)}, bf16[384,896]{1,0:T(8,128)(2,1)S(1)}, u32[]{:S(2)}, u32[]{:S(2)}) collective-permute-start(bf16[384,896]{1,0:T(8,128)(2,1)S(1)} %get-tuple-element.65), channel_id=1, source_target_pairs={{0,1},{1,2},{2,3},{4,5},{5,6},{6,7},{8,9},{9,10},{10,11},{12,13},{... | collective-permute-start | bytes 2064392 | tf_op jit(solution)/shard_map/ppermute | solution.py:87
  291.3 6.7 %collective-permute-start.21 = (bf16[384,896]{1,0:T(8,128)(2,1)S(1)}, bf16[384,896]{1,0:T(8,128)(2,1)S(1)}, u32[]{:S(2)}, u32[]{:S(2)}) collective-permute-start(bf16[384,896]{1,0:T(8,128)(2,1)S(1)} %add_convert_fusion.2), channel_id=1, source_target_pairs={{0,1},{1,2},{4,5},{5,6},{8,9},{9,10},{12,13},{13,14},{16,17},{17,1... | collective-permute-start | bytes 2064392 | tf_op jit(solution)/shard_map/ppermute | solution.py:78
  300.6 6.1 %collective-permute-done.17 = bf16[384,896]{1,0:T(8,128)(2,1)S(1)} collective-permute-done((bf16[384,896]{1,0:T(8,128)(2,1)S(1)}, bf16[384,896]{1,0:T(8,128)(2,1)S(1)}, u32[]{:S(2)}, u32[]{:S(2)}) %collective-permute-start.17) | collective-permute-done | bytes 688160 | tf_op jit(solution)/shard_map/ppermute | solution.py:87
  306.9 9.9 %collective-permute-done.21 = bf16[384,896]{1,0:T(8,128)(2,1)S(1)} collective-permute-done((bf16[384,896]{1,0:T(8,128)(2,1)S(1)}, bf16[384,896]{1,0:T(8,128)(2,1)S(1)}, u32[]{:S(2)}, u32[]{:S(2)}) %collective-permute-start.21) | collective-permute-done | bytes 688160 | tf_op jit(solution)/shard_map/ppermute | solution.py:78
  318.6 8.4 %collective-permute-start.22 = (bf16[384,896]{1,0:T(8,128)(2,1)S(1)}, bf16[384,896]{1,0:T(8,128)(2,1)S(1)}, u32[]{:S(2)}, u32[]{:S(2)}) collective-permute-start(bf16[384,896]{1,0:T(8,128)(2,1)S(1)} %get-tuple-element.63), channel_id=1, source_target_pairs={{0,1},{1,2},{2,3},{4,5},{5,6},{6,7},{8,9},{9,10},{10,11},{12,13},{... | collective-permute-start | bytes 2064392 | tf_op jit(solution)/shard_map/ppermute | solution.py:87
  327.8 9.4 %collective-permute-done.24 = bf16[384,896]{1,0:T(8,128)(2,1)S(1)} collective-permute-done((bf16[384,896]{1,0:T(8,128)(2,1)S(1)}, bf16[384,896]{1,0:T(8,128)(2,1)S(1)}, u32[]{:S(2)}, u32[]{:S(2)}) %collective-permute-start.24) | collective-permute-done | bytes 688160 | tf_op jit(solution)/shard_map/ppermute | solution.py:88
  (227 shorter events, 104.8 us)
Async XLA Ops:
  7.2 113.5 %all-gather.4.cloned.1.call-start = ((), (), s32[]{:S(2)}) async-start(), calls=%async_computation.3 | async-start | bytes 4587520 | tf_op jit(solution)/shard_map/all_gather | solution.py:321
  9.6 181.7 %all-gather.8.cloned.1.call-start = ((), (), s32[]{:S(2)}) async-start(), calls=%async_computation.5 | async-start | bytes 4128768 | tf_op jit(solution)/shard_map/all_gather | solution.py:383
  10.3 190.4 %all-gather.6.cloned.1.call-start = ((), (), s32[]{:S(2)}) async-start(), calls=%async_computation.4 | async-start | bytes 6193152 | tf_op jit(solution)/shard_map/all_gather | solution.py:380
  23.9 53.1 %all-to-all-start.1 = ((bf16[32,72,896]{2,1,0:T(8,128)(2,1)}), bf16[32,72,896]{2,1,0:T(8,128)(2,1)}, u32[]{:S(2)}, u32[]{:S(2)}) async-start(bf16[32,72,896]{2,1,0:T(8,128)(2,1)} %gather_fusion), calls=%async_computation.1 | async-start | bytes 8257536 | tf_op jit(solution)/shard_map/all_to_all | solution.py:335
  28.6 311.5 %reduce-scatter.2.cloned.1.call-start = ((), (), s32[]{:S(2)}) async-start(), calls=%async_computation.6 | async-start | bytes 10321920 | tf_op jit(solution)/shard_map/reduce_scatter | solution.py:438
  28.7 24.0 %collective-permute-start.1 = (bf16[256,896]{1,0:T(8,128)(2,1)S(1)}, bf16[256,896]{1,0:T(8,128)(2,1)S(1)}, u32[]{:S(2)}, u32[]{:S(2)}) collective-permute-start(bf16[256,896]{1,0:T(8,128)(2,1)S(1)} %slice.95.refs_8_), channel_id=1, source_target_pairs={{0,1},{1,2},{2,3},{4,5},{5,6},{6,7},{8,9},{9,10},{10,11},{12,13},{... | collective-permute-start | bytes 1376264 | tf_op jit(solution)/shard_map/ppermute | solution.py:45
  32.2 34.7 %collective-permute-start.3 = (bf16[256,896]{1,0:T(8,128)(2,1)S(1)}, bf16[256,896]{1,0:T(8,128)(2,1)S(1)}, u32[]{:S(2)}, u32[]{:S(2)}) collective-permute-start(bf16[256,896]{1,0:T(8,128)(2,1)S(1)} %slice.95.refs_8_), channel_id=1, source_target_pairs={{1,0},{2,1},{3,2},{5,4},{6,5},{7,6},{9,8},{10,9},{11,10},{13,12},{... | collective-permute-start | bytes 1376264 | tf_op jit(solution)/shard_map/ppermute | solution.py:45
  52.7 35.8 %collective-permute-start.2 = (bf16[256,896]{1,0:T(8,128)(2,1)S(1)}, bf16[256,896]{1,0:T(8,128)(2,1)}, u32[]{:S(2)}, u32[]{:S(2)}) collective-permute-start(bf16[256,896]{1,0:T(8,128)(2,1)S(1)} %collective-permute-done.1), channel_id=1, source_target_pairs={{1,2},{2,3},{5,6},{6,7},{9,10},{10,11},{13,14},{14,15},{17,18},{18... | collective-permute-start | bytes 1376264 | tf_op jit(solution)/shard_map/ppermute | solution.py:49
  67.0 32.6 %collective-permute-start.4 = (bf16[256,896]{1,0:T(8,128)(2,1)S(1)}, bf16[256,896]{1,0:T(8,128)(2,1)}, u32[]{:S(2)}, u32[]{:S(2)}) collective-permute-start(bf16[256,896]{1,0:T(8,128)(2,1)S(1)} %collective-permute-done.3), channel_id=1, source_target_pairs={{1,0},{2,1},{5,4},{6,5},{9,8},{10,9},{13,12},{14,13},{17,16},{18,1... | collective-permute-start | bytes 1376264 | tf_op jit(solution)/shard_map/ppermute | solution.py:50
  102.9 36.1 %collective-permute-start.5 = (bf16[512,896]{1,0:T(8,128)(2,1)S(1)}, bf16[512,896]{1,0:T(8,128)(2,1)}, u32[]{:S(2)}, u32[]{:S(2)}) collective-permute-start(bf16[512,896]{1,0:T(8,128)(2,1)S(1)} %slice.118.refs_0_), channel_id=1, source_target_pairs={{1,0},{2,1},{3,2},{5,4},{6,5},{7,6},{9,8},{10,9},{11,10},{13,12},{... | collective-permute-start | bytes 2752520 | tf_op jit(solution)/shard_map/ppermute | solution.py:45
  104.2 45.7 %collective-permute-start.6 = (bf16[512,896]{1,0:T(8,128)(2,1)S(1)}, bf16[512,896]{1,0:T(8,128)(2,1)}, u32[]{:S(2)}, u32[]{:S(2)}) collective-permute-start(bf16[512,896]{1,0:T(8,128)(2,1)S(1)} %slice.118.refs_0_), channel_id=1, source_target_pairs={{0,1},{1,2},{2,3},{4,5},{5,6},{6,7},{8,9},{9,10},{10,11},{12,13},{... | collective-permute-start | bytes 2752520 | tf_op jit(solution)/shard_map/ppermute | solution.py:45
  119.4 29.5 %collective-permute-start.9 = (bf16[256,896]{1,0:T(8,128)(2,1)}, bf16[256,896]{1,0:T(8,128)(2,1)}, u32[]{:S(2)}, u32[]{:S(2)}) collective-permute-start(bf16[256,896]{1,0:T(8,128)(2,1)} %collective-permute-done.8), channel_id=1, source_target_pairs={{1,0},{2,1},{5,4},{6,5},{9,8},{10,9},{13,12},{14,13},{17,16},{18,1... | collective-permute-start | bytes 1376264 | tf_op jit(solution)/shard_map/ppermute | solution.py:50
  120.7 28.2 %collective-permute-start.7 = (bf16[256,896]{1,0:T(8,128)(2,1)S(1)}, bf16[256,896]{1,0:T(8,128)(2,1)S(1)}, u32[]{:S(2)}, u32[]{:S(2)}) collective-permute-start(bf16[256,896]{1,0:T(8,128)(2,1)S(1)} %collective-permute-done), channel_id=1, source_target_pairs={{1,2},{2,3},{5,6},{6,7},{9,10},{10,11},{13,14},{14,15},{17,18},{18... | collective-permute-start | bytes 1376264 | tf_op jit(solution)/shard_map/ppermute | solution.py:49
  121.4 37.2 %collective-permute-start.12 = (bf16[256,896]{1,0:T(8,128)(2,1)}, bf16[256,896]{1,0:T(8,128)(2,1)S(1)}, u32[]{:S(2)}, u32[]{:S(2)}) collective-permute-start(bf16[256,896]{1,0:T(8,128)(2,1)} %broadcast_select_fusion.5.refs_10_), channel_id=1, source_target_pairs={{2,3},{1,0},{6,7},{5,4},{10,11},{9,8},{14,15},{13,12},{18,19},{17,... | collective-permute-start | bytes 1376264 | tf_op jit(solution)/shard_map/ppermute | solution.py:55
  139.0 48.4 %collective-permute-start.11 = (bf16[512,896]{1,0:T(8,128)(2,1)}, bf16[512,896]{1,0:T(8,128)(2,1)}, u32[]{:S(2)}, u32[]{:S(2)}) collective-permute-start(bf16[512,896]{1,0:T(8,128)(2,1)} %collective-permute-done.5), channel_id=1, source_target_pairs={{1,0},{2,1},{5,4},{6,5},{9,8},{10,9},{13,12},{14,13},{17,16},{18,1... | collective-permute-start | bytes 2752520 | tf_op jit(solution)/shard_map/ppermute | solution.py:50
  150.0 37.5 %collective-permute-start.10 = (bf16[512,896]{1,0:T(8,128)(2,1)}, bf16[512,896]{1,0:T(8,128)(2,1)}, u32[]{:S(2)}, u32[]{:S(2)}) collective-permute-start(bf16[512,896]{1,0:T(8,128)(2,1)} %collective-permute-done.6), channel_id=1, source_target_pairs={{1,2},{2,3},{5,6},{6,7},{9,10},{10,11},{13,14},{14,15},{17,18},{18... | collective-permute-start | bytes 2752520 | tf_op jit(solution)/shard_map/ppermute | solution.py:49
  159.4 26.0 %collective-permute-start.13 = (bf16[256,896]{1,0:T(8,128)(2,1)S(1)}, bf16[256,896]{1,0:T(8,128)(2,1)S(1)}, u32[]{:S(2)}, u32[]{:S(2)}) collective-permute-start(bf16[256,896]{1,0:T(8,128)(2,1)S(1)} %broadcast_select_fusion.4.refs_2_.refs_6_), channel_id=1, source_target_pairs={{2,3},{1,0},{6,7},{5,4},{10,11},{9,8},{14,15},{13,12},{18,19},{17,... | collective-permute-start | bytes 1376264 | tf_op jit(solution)/shard_map/ppermute | solution.py:55
  189.7 22.1 %collective-permute-start.14 = (bf16[512,896]{1,0:T(8,128)(2,1)}, bf16[512,896]{1,0:T(8,128)(2,1)}, u32[]{:S(2)}, u32[]{:S(2)}) collective-permute-start(bf16[512,896]{1,0:T(8,128)(2,1)} %broadcast_select_fusion.1.refs_2_), channel_id=1, source_target_pairs={{2,3},{1,0},{6,7},{5,4},{10,11},{9,8},{14,15},{13,12},{18,19},{17,... | collective-permute-start | bytes 2752520 | tf_op jit(solution)/shard_map/ppermute | solution.py:55
  226.7 22.5 %collective-permute-start.15 = (bf16[384,896]{1,0:T(8,128)(2,1)}, bf16[384,896]{1,0:T(8,128)(2,1)}, u32[]{:S(2)}, u32[]{:S(2)}) collective-permute-start(bf16[384,896]{1,0:T(8,128)(2,1)} %subtract_convert_fusion.5), channel_id=1, source_target_pairs={{3,2},{0,1},{7,6},{4,5},{11,10},{8,9},{15,14},{12,13},{19,18},{16,... | collective-permute-start | bytes 2064392 | tf_op jit(solution)/shard_map/ppermute | solution.py:70
  255.2 26.9 %collective-permute-start.16 = (bf16[384,896]{1,0:T(8,128)(2,1)S(1)}, bf16[384,896]{1,0:T(8,128)(2,1)S(1)}, u32[]{:S(2)}, u32[]{:S(2)}) collective-permute-start(bf16[384,896]{1,0:T(8,128)(2,1)S(1)} %add_convert_fusion.5), channel_id=1, source_target_pairs={{0,1},{1,2},{4,5},{5,6},{8,9},{9,10},{12,13},{13,14},{16,17},{17,1... | collective-permute-start | bytes 2064392 | tf_op jit(solution)/shard_map/ppermute | solution.py:78
  256.5 25.5 %collective-permute-start.18 = (bf16[384,896]{1,0:T(8,128)(2,1)S(1)}, bf16[384,896]{1,0:T(8,128)(2,1)S(1)}, u32[]{:S(2)}, u32[]{:S(2)}) collective-permute-start(bf16[384,896]{1,0:T(8,128)(2,1)S(1)} %add_convert_fusion.5), channel_id=1, source_target_pairs={{3,2},{2,1},{7,6},{6,5},{11,10},{10,9},{15,14},{14,13},{19,18},{18... | collective-permute-start | bytes 2064392 | tf_op jit(solution)/shard_map/ppermute | solution.py:78
  285.6 21.2 %collective-permute-start.17 = (bf16[384,896]{1,0:T(8,128)(2,1)S(1)}, bf16[384,896]{1,0:T(8,128)(2,1)S(1)}, u32[]{:S(2)}, u32[]{:S(2)}) collective-permute-start(bf16[384,896]{1,0:T(8,128)(2,1)S(1)} %get-tuple-element.65), channel_id=1, source_target_pairs={{0,1},{1,2},{2,3},{4,5},{5,6},{6,7},{8,9},{9,10},{10,11},{12,13},{... | collective-permute-start | bytes 2064392 | tf_op jit(solution)/shard_map/ppermute | solution.py:87
  291.3 25.6 %collective-permute-start.21 = (bf16[384,896]{1,0:T(8,128)(2,1)S(1)}, bf16[384,896]{1,0:T(8,128)(2,1)S(1)}, u32[]{:S(2)}, u32[]{:S(2)}) collective-permute-start(bf16[384,896]{1,0:T(8,128)(2,1)S(1)} %add_convert_fusion.2), channel_id=1, source_target_pairs={{0,1},{1,2},{4,5},{5,6},{8,9},{9,10},{12,13},{13,14},{16,17},{17,1... | collective-permute-start | bytes 2064392 | tf_op jit(solution)/shard_map/ppermute | solution.py:78
  317.3 20.0 %collective-permute-start.24 = (bf16[384,896]{1,0:T(8,128)(2,1)S(1)}, bf16[384,896]{1,0:T(8,128)(2,1)S(1)}, u32[]{:S(2)}, u32[]{:S(2)}) collective-permute-start(bf16[384,896]{1,0:T(8,128)(2,1)S(1)} %get-tuple-element.64), channel_id=1, source_target_pairs={{1,0},{2,1},{3,2},{5,4},{6,5},{7,6},{9,8},{10,9},{11,10},{13,12},{... | collective-permute-start | bytes 2064392 | tf_op jit(solution)/shard_map/ppermute | solution.py:88
  (57 other events, 728.3 us)
Sparse Core Ops, SparseCore 0:
  9.6 94.1 all-gather.3
  105.7 34.5 all-gather.7
  142.2 42.2 all-gather.5
  249.4 77.3 reduce-scatter.1
